TPU v7x, 256 devices: a whole 4x4x8 slice. The times are simulated.
256 devices in a mesh: reg: 32 (over z, x_lo, core), glob: 4 (over y), cpl: 2 (over x_hi).
Axes of the slice: x: 4 (x_hi: 2, x_lo: 2; x = x_hi * 2 + x_lo), y: 4, z: 8, core: 2. Of those that a mesh axis runs over, the one named last changes fastest.
Arguments:
- saved_input: bfloat16 [2, 172, 512, 512], P('cpl', None, 'reg', 'glob'), may hold values from -6 to 6
- pre_act: bfloat16 [2, 128, 512, 512], P('cpl', None, 'reg', 'glob'), may hold values from -8 to 8
- cotangent: bfloat16 [2, 128, 512, 512], P('cpl', None, 'reg', 'glob'), may hold values from -6 to 6
- conv_weight: bfloat16 [9, 172, 128], replicated, may hold values from -0.15625 to 0.15625
- interp: bfloat16 [4, 512, 128, 128], P('glob', 'reg'), may hold values from -0.5 to 0.5
- targets: int32 [4, 512], P('glob', 'reg'), may hold values from 0 to 255, as said below
- noise_index: int32 [2], P('cpl'), may hold values from 0 to 17
Outputs:
- input_grad: bfloat16 [2, 99, 512, 512], P('cpl', None, 'reg', 'glob')
- weight_grad: float32 [9, 172, 128], replicated
- bias_grad: float32 [128], replicated
- global_grad: float32 [256, 73, 128], P(('reg', 'glob'))
Inputs may be any that keep to these rules, and one draw needn't show every extreme that they name: `targets`: with h = ((r // 16) * 4 + g) * 2, row block (g, r) reads a global block h - 1 to h + 2 modulo 256, except that the second of every 16 rows reads block h + 256 // 2 modulo 256; the first of every 16 rows reads h - 1 and the last reads h + 2.
All inputs are finite; a program needn't handle non-finite values.
Results may differ from a plain program's by a relative error of at most 0.0054.
Values may be sent and summed in bfloat16 or wider, within the bound.
A program may use at most 128 MiB of HBM per device.

v0:
```python
import math

import jax
import jax.numpy as jnp
from jax import lax
from jax.sharding import PartitionSpec as P

CG = 73
GPTS = 128
GB_DEV = 2
NOISE_LEVELS = 18


def padded_2(cells, sides, width):
    for axis, dim in sides:
        count = lax.axis_size(axis)
        ends = count - 1
        head = lax.slice_in_dim(cells, 0, width, axis=dim)
        tail = lax.slice_in_dim(cells, cells.shape[dim] - width, cells.shape[dim], axis=dim)
        cells = jnp.concatenate(
            [
                lax.ppermute(tail, axis, [(i, (i + 1) % count) for i in range(ends)]),
                cells,
                lax.ppermute(head, axis, [((i + 1) % count, i) for i in range(ends)]),
            ],
            axis=dim,
        )
    return cells


def noise_scale(index):
    frac = index.astype(jnp.float32) / (NOISE_LEVELS - 1)
    sigma = jnp.exp(jnp.log(2.0) + frac * (jnp.log(0.05) - jnp.log(2.0)))
    return 1.0 / jnp.sqrt(sigma * sigma + 0.25)


def body(saved_input, pre_act, cotangent, conv_weight, interp, targets, noise_index):
    channels_in = saved_input.shape[1]
    tile_rows = saved_input.shape[2]
    tile_cols = saved_input.shape[3]
    hidden = pre_act.shape[1]
    regional = channels_in - CG
    pre = pre_act[0].astype(jnp.float32)
    sig = jax.nn.sigmoid(pre)
    dz32 = cotangent[0].astype(jnp.float32) * sig * (1.0 + pre * (1.0 - sig))
    padded = padded_2(dz32.astype(jnp.bfloat16), (("reg", 1), ("glob", 2)), 1)
    pieces = []
    for offset in range(9):
        shift_row = offset // 3 - 1
        shift_col = offset % 3 - 1
        pieces.append(
            padded[
                :,
                1 - shift_row : 1 - shift_row + tile_rows,
                1 - shift_col : 1 - shift_col + tile_cols,
            ]
        )
    stacked = jnp.stack(pieces, 0).reshape(9 * hidden, tile_rows * tile_cols)
    w_flat = jnp.transpose(conv_weight, (1, 0, 2)).reshape(channels_in, 9 * hidden)
    back = jnp.dot(w_flat, stacked, preferred_element_type=jnp.float32)
    inputs = saved_input[0].reshape(channels_in, tile_rows * tile_cols)
    weight_term = lax.dot_general(
        inputs, stacked, (((1,), (1,)), ((), ())), preferred_element_type=jnp.float32
    )
    weight_term = jnp.transpose(weight_term.reshape(channels_in, 9, hidden), (1, 0, 2))
    weight_total, bias_total = lax.psum(
        (weight_term, jnp.sum(dz32, axis=(1, 2))), ("reg", "glob", "cpl")
    )
    points = (
        lax.axis_size("reg") * tile_rows * lax.axis_size("glob") * tile_cols * lax.axis_size("cpl")
    )
    scale_norm = 1.0 / math.sqrt(points)
    input_grad = (
        (noise_scale(noise_index[0]) * back[:regional])
        .reshape(regional, tile_rows, tile_cols)
        .astype(jnp.bfloat16)[None]
    )
    cond = back[regional:].astype(jnp.bfloat16).reshape(CG, tile_rows, tile_cols)
    contrib = jnp.einsum(
        "crt,rtj->rcj", cond, interp[0], preferred_element_type=jnp.float32
    ).reshape(tile_rows, CG * GPTS)
    local_targets = targets[0]
    wanted = lax.broadcasted_iota(
        jnp.int32, (GB_DEV * lax.axis_size(("reg", "glob")), tile_rows), 0
    )
    selector = (wanted == local_targets[None, :]).astype(jnp.float32)
    summed = jnp.dot(
        selector, contrib, precision=lax.Precision.HIGHEST, preferred_element_type=jnp.float32
    )
    owned = lax.psum_scatter(
        summed.reshape(GB_DEV * lax.axis_size(("reg", "glob")), CG, GPTS),
        ("reg", "glob"),
        scatter_dimension=0,
        tiled=True,
    )
    global_grad = lax.psum(owned, "cpl")
    return (input_grad, weight_total * scale_norm, bias_total * scale_norm, global_grad)


def solution(mesh):
    in_specs = (
        P("cpl", None, "reg", "glob"),
        P("cpl", None, "reg", "glob"),
        P("cpl", None, "reg", "glob"),
        P(),
        P("glob", "reg", None, None),
        P("glob", "reg"),
        P("cpl"),
    )
    out_specs = (P("cpl", None, "reg", "glob"), P(), P(), P(("reg", "glob"), None, None))
    return jax.shard_map(body, mesh=mesh, in_specs=in_specs, out_specs=out_specs, check_vma=False)
```

profile of v0, /device:TPU:1, one launch (start us, length us, event | category | flops | bytes accessed | tf_op | source)
XLA Modules:
  0.0 1477.3 jit_solution(2412062715809341341)
XLA Ops:
  7.2 1.8 copy.51
  9.1 1.7 copy.50
  11.4 5.1 collective-permute-start.1
  16.5 1.9 collective-permute-start
  18.5 1.3 collective-permute-done
  19.8 2.6 collective-permute-start.3
  22.3 1.3 collective-permute-start.2
  24.1 2.6 collective-permute-done.2
  26.7 0.7 maximum_maximum_fusion
  27.4 1.0 fusion.40
  28.4 1.1 fusion.39
  29.5 1.0 fusion.37
  30.5 1.0 fusion.36
  31.6 1.2 fusion.30
  32.8 1.0 fusion.35
  33.8 0.8 fusion.34
  34.7 1.0 fusion.33
  35.6 0.8 fusion.31
  36.5 7.4 copy.52
  43.9 3.5 fusion.6
  47.9 6.4 fusion.27
  57.0 82.6 %psum.22 = f32[128]{0:T(128)S(1)} all-reduce(f32[128]{0:T(128)S(1)} %get-tuple-element.20), channel_id=1, replica_groups=mesh['reg'=32,'glob'=4,'cpl'=2] {'reg','glob','cpl'}, use_global_device_ids=true, to_apply=%region_2.0 | all-reduce | flops 128 | bytes 1024 | tf_op jit(solution)/shard_map/psum | solution.py:66
  140.1 4.0 fusion.9
  144.2 1.2 reshape.49
  145.6 0.8 slice_bitcast_fusion.6
  146.4 1023.8 %all-reduce.9.cloned.1.call-done = f32[256,73,128]{2,0,1:T(8,128)} async-done(((f32[256,73,128]{2,0,1:T(8,128)}), f32[256,73,128]{2,0,1:T(8,128)}) %all-reduce.9.cloned.1.call-update) | async-done | bytes 9568272
  1170.2 1.6 constant_dynamic-slice_fusion
  1171.8 260.5 %all-reduce.5.cloned.1.call-done = f32[9,172,128]{2,0,1:T(8,128)} async-done(((f32[9,172,128]{2,0,1:T(8,128)}), f32[9,172,128]{2,0,1:T(8,128)}) %all-reduce.5.cloned.1.call-update) | async-done | bytes 792592 | tf_op jit(solution)/shard_map/psum | solution.py:66
  1432.3 1.5 broadcast_multiply_fusion
  1433.8 1.1 copy.56
  1434.9 34.3 %all-reduce.7.cloned.1.call-done = f32[2,73,128]{2,0,1:T(2,128)} async-done(((f32[2,73,128]{2,0,1:T(2,128)}), f32[2,73,128]{2,0,1:T(2,128)}) %all-reduce.7.cloned.1.call-update) | async-done | bytes 74768 | tf_op jit(solution)/shard_map/psum | solution.py:96
  1469.3 1.5 copy.99
  (34 shorter events, 3.4 us)
Async XLA Ops:
  7.2 40.4 %copy-start = (bf16[1,16,128,128]{3,2,1,0:T(8,128)(2,1)S(1)}, bf16[1,16,128,128]{3,2,1,0:T(8,128)(2,1)}, u32[]{:S(2)}) copy-start(bf16[1,16,128,128]{3,2,1,0:T(8,128)(2,1)} %param.11) | copy-start | bytes 1572868
  7.2 16.5 %copy-start.2 = (bf16[9,172,128]{2,1,0:T(8,128)(2,1)S(1)}, bf16[9,172,128]{2,1,0:T(8,128)(2,1)}, u32[]{:S(2)}) copy-start(bf16[9,172,128]{2,1,0:T(8,128)(2,1)} %param.10) | copy-start | bytes 1188868
  7.2 1163.0 %all-reduce.9.cloned.1.call-start = ((), (), s32[]{:S(2)}) async-start(), calls=%async_computation.2 | async-start | bytes 19136512
  11.4 7.1 collective-permute-start.1
  16.5 3.2 collective-permute-start
  19.8 4.3 collective-permute-start.3
  22.3 4.4 collective-permute-start.2
  43.9 4.0 copy-start.3
  54.3 1.1 copy-start.1
  54.3 1.5 copy-start.4
  54.3 1378.0 %all-reduce.5.cloned.1.call-start = ((), (), s32[]{:S(2)}) async-start(), calls=%async_computation | async-start | bytes 2818048 | tf_op jit(solution)/shard_map/psum | solution.py:66
  145.4 1323.8 %all-reduce.7.cloned.1.call-start = ((), (), s32[]{:S(2)}) async-start(), calls=%async_computation.1 | async-start | bytes 149504 | tf_op jit(solution)/shard_map/psum | solution.py:96
Sparse Core Ops, SparseCore 0:
  54.5 1115.6 all-reduce.8
  1175.6 256.6 all-reduce.4
  1435.6 33.5 all-reduce.6
where the time goes:
time: 1480 us
  waiting for transfers between devices  1320 us (89%)
  blocking collectives  82.6 us (6%)
  local copies, waits for them, and re-layouts  24.9 us (2%)
  between operations  15.4 us (1%)
    unnamed x4, waiting for transfers between devices  1020 us
    psum x1, waiting for transfers between devices, body(): lax.psum((weight_term, jnp.sum(dz32, axis=(1, 2))), ('reg', 'glob', 'cpl'))  260 us
    psum x1, blocking collectives, body(): lax.psum((weight_term, jnp.sum(dz32, axis=(1, 2))), ('reg', 'glob', 'cpl'))  82.6 us
    psum x1, waiting for transfers between devices, body(): global_grad = lax.psum(owned, 'cpl')  34.3 us
  transfers between devices with their start and end apart: 7, of which 5 were waited for; matrix products, arithmetic and copies ran while one was open for 1% of the time, Pallas kernels for 0%

commit v1 on v0

v1 whole, which is shorter than its diff:
```python
import math

import jax
import jax.numpy as jnp
from jax import lax
from jax.experimental import pallas as pl
from jax.experimental.pallas import tpu as pltpu
from jax.sharding import PartitionSpec as P

CH = 128
CR = 99
CG = 73
CIN = 172
CPAD = 176
HALF = 88
TR = 16
TC = 128
NGB = 256
NOISE_LEVELS = 18
PIECE = 56
PIECE_B = 64
ROWS_HALF = 9 * HALF
ROWS_ALL = 16 * PIECE
TOP = 8
PITCH = TOP + TC + 8
BLK = 80
SCALE_NORM = 1.0 / math.sqrt(512 * 512 * 2)
MESH = pl.DeviceIdType.MESH
F32 = jnp.float32
BF16 = jnp.bfloat16


def kernel(
    saved_hbm, pre_hbm, cot_hbm, w_hbm, interp_hbm, targets_ref, noise_ref,
    igrad_hbm, wgrad_ref, bgrad_ref, ggrad_ref,
    saved_v, pre_v, cot_v, w_v, interp_v,
    d32, s32, p32, dzc, smat, wcat, colbuf, colrecv, corner,
    awh, crecv, acc, xrecv, zbuf, fbuf, gbuf,
    bk32, cmask, glob_out, glob_recv, own, cplrecv, ig_v,
    in_sem, halo_ss, halo_rs, core_ss, core_rs, xy_ss, xy_rs, z_ss, z_rs,
    ag_ss, ag_rs, fw_ss, fw_rs, gl_ss, gl_rs, out_sem,
):
    reg = lax.axis_index("reg")
    glob = lax.axis_index("glob")
    cpl = lax.axis_index("cpl")
    z = reg // 4
    x_lo = (reg // 2) % 2
    core = reg % 2
    x = cpl * 2 + x_lo
    y = glob
    q = x * 4 + y

    def at(x_, y_, z_, core_):
        return {"reg": z_ * 4 + (x_ % 2) * 2 + core_, "glob": y_, "cpl": x_ // 2}

    def plane(d):
        return (x + d // 4) % 4, (y + d % 4) % 4

    def plane_dev(d):
        px, py = plane(d)
        return at(px, py, z, core)

    def z_dev(d):
        return at(x, y, (z + d) % 8, core)

    def halo_dev(dr, dg):
        return {"reg": (reg + dr + 32) % 32, "glob": (glob + dg + 4) % 4, "cpl": cpl}

    def flat_dev(step):
        flat = (reg * 4 + glob + step + 128) % 128
        return {"reg": flat // 4, "glob": flat % 4, "cpl": cpl}

    sibling = at(x, y, z, 1 - core)
    other = {"reg": reg, "glob": glob, "cpl": 1 - cpl}

    loads = [
        pltpu.make_async_copy(src, dst, in_sem.at[n])
        for n, (src, dst) in enumerate((
            (pre_hbm.at[0], pre_v),
            (cot_hbm.at[0], cot_v),
            (saved_hbm.at[0], saved_v),
            (w_hbm, w_v),
            (interp_hbm.at[0], interp_v),
        ))
    ]
    for load in loads:
        load.start()

    barrier = pltpu.get_barrier_semaphore()

    def greet(device):
        pl.semaphore_signal(barrier, inc=1, device_id=device, device_id_type=MESH)

    halo_steps = [(dr, dg) for dr in (-1, 0, 1) for dg in (-1, 0, 1) if dr or dg]
    for dr, dg in halo_steps:
        greet(halo_dev(dr, dg))
    for step in (-1, 1, 64):
        greet(flat_dev(step))
    greet(other)
    greet(sibling)
    lax.fori_loop(1, 16, lambda d, c: (greet(plane_dev(d)), c)[1], 0)
    lax.fori_loop(1, 8, lambda d, c: (greet(z_dev(d)), c)[1], 0)

    s32[CIN * TR :, :] = jnp.zeros((CPAD * TR - CIN * TR, TC), F32)
    wcat[:, CPAD - 16 :, :] = jnp.zeros((3, 16, 3 * CH), BF16)
    acc[ROWS_HALF:, :] = jnp.zeros((ROWS_ALL - ROWS_HALF, CH), F32)
    bk32[:, CPAD:, :] = jnp.zeros((TR, 8, TC), F32)

    loads[0].wait()
    loads[1].wait()

    def silu_step(n, carry):
        pre = pre_v[pl.ds(n * 8, 8)].astype(F32)
        cot = cot_v[pl.ds(n * 8, 8)].astype(F32)
        sig = 0.5 * jnp.tanh(0.5 * pre) + 0.5
        dz = cot * sig * (1.0 + pre * (1.0 - sig))
        d32[pl.ds(pl.multiple_of(n * 8 * TR, 128), 8 * TR), :] = dz.reshape(8 * TR, TC)
        return carry

    lax.fori_loop(0, CH // 8, silu_step, 0)

    def turn(i):
        tile = jnp.transpose(d32[pl.ds(i, CH, stride=TR), :], (1, 0))
        p32[i + 1, TOP : TOP + TC, :] = tile
        colbuf[0, i : i + 1, :] = tile[:1]
        colbuf[1, i : i + 1, :] = tile[TC - 1 :]
        return tile

    total = jnp.zeros((TC, CH), F32)
    for i in range(TR):
        total = total + turn(i)
    bias = jnp.sum(total, axis=0, keepdims=True)

    pl.semaphore_wait(barrier, 8 + 3 + 1 + 1 + 15 + 7)

    halo = []
    for n, (dr, dg) in enumerate(halo_steps):
        row = TR if dr > 0 else 1
        if dg == 0:
            src = p32.at[row, pl.ds(TOP, TC)]
            dst = p32.at[0 if dr > 0 else TR + 1, pl.ds(TOP, TC)]
        elif dr == 0:
            src = colbuf.at[1 if dg > 0 else 0]
            dst = colrecv.at[0 if dg > 0 else 1]
        else:
            src = p32.at[row, pl.ds(TOP + TC - 8 if dg > 0 else TOP, 8)]
            dst = corner.at[0 if dr > 0 else 1, 0 if dg > 0 else 1]
        copy = pltpu.make_async_remote_copy(
            src, dst, halo_ss.at[n], halo_rs.at[n],
            device_id=halo_dev(dr, dg), device_id_type=MESH,
        )
        copy.start()
        halo.append(copy)

    loads[2].wait()

    def saved_step(n, carry):
        part = saved_v[pl.ds(n * 4, 4)].astype(F32)
        s32[pl.ds(pl.multiple_of(n * 4 * TR, 64), 4 * TR), :] = part.reshape(4 * TR, TC)
        return carry

    lax.fori_loop(0, CIN // 4, saved_step, 0)
    for i in range(TR):
        smat[:, i * TC : (i + 1) * TC] = s32[pl.ds(i, CPAD, stride=TR), :].astype(BF16)

    def shift_rows(i):
        for bi in range(3):
            dzc[pl.ds(pl.multiple_of(i * TC, TC), TC), bi * CH : (bi + 1) * CH] = p32[
                i, TOP + 1 - bi : TOP + 1 - bi + TC, :
            ].astype(BF16)

    loads[3].wait()
    for a in range(3):
        for bi in range(3):
            wcat[a, :CIN, bi * CH : (bi + 1) * CH] = w_v[3 * a + bi]

    for copy in halo:
        copy.wait_recv()
    up = (reg > 0).astype(F32)
    down = (reg < 31).astype(F32)
    left = (glob > 0).astype(F32)
    right = (glob < 3).astype(F32)
    p32[0, TOP : TOP + TC, :] = p32[0, TOP : TOP + TC, :] * up
    p32[TR + 1, TOP : TOP + TC, :] = p32[TR + 1, TOP : TOP + TC, :] * down
    for i in range(TR):
        p32[i + 1, TOP - 1 : TOP, :] = colrecv[0, i : i + 1, :] * left
        p32[i + 1, TOP + TC : TOP + TC + 1, :] = colrecv[1, i : i + 1, :] * right
    p32[0, TOP - 1 : TOP, :] = corner[0, 0, 7:8, :] * (up * left)
    p32[0, TOP + TC : TOP + TC + 1, :] = corner[0, 1, 0:1, :] * (up * right)
    p32[TR + 1, TOP - 1 : TOP, :] = corner[1, 0, 7:8, :] * (down * left)
    p32[TR + 1, TOP + TC : TOP + TC + 1, :] = corner[1, 1, 0:1, :] * (down * right)

    lax.fori_loop(0, TR + 2, lambda i, c: (shift_rows(i), c)[1], 0)

    core_copies = []
    for a in range(3):
        term = jnp.dot(
            smat[...], dzc[(2 - a) * TC : (2 - a) * TC + TR * TC, :],
            preferred_element_type=F32,
        )
        for bi in range(3):
            k = 3 * a + bi
            for h in range(2):
                awh[h, k * HALF : (k + 1) * HALF, :] = term[
                    h * HALF : (h + 1) * HALF, bi * CH : (bi + 1) * CH
                ]
        if a == 0:
            awh[1, CIN - HALF : CIN - HALF + 1, :] = bias
        rows = pl.ds(3 * a * HALF, 3 * HALF)
        copy = pltpu.make_async_remote_copy(
            awh.at[1 - core, rows], crecv.at[rows], core_ss.at[a], core_rs.at[a],
            device_id=sibling, device_id_type=MESH,
        )
        copy.start()
        core_copies.append(copy)
    for a in range(3):
        core_copies[a].wait_recv()
        rows = pl.ds(3 * a * HALF, 3 * HALF)
        acc[rows, :] = awh[core, rows, :] + crecv[rows, :]

    def xy_copy(d):
        px, py = plane(d)
        return pltpu.make_async_remote_copy(
            acc.at[pl.ds(pl.multiple_of((px * 4 + py) * PIECE, 8), PIECE)],
            xrecv.at[d], xy_ss.at[d], xy_rs.at[d],
            device_id=at(px, py, z, core), device_id_type=MESH,
        )

    lax.fori_loop(0, 15, lambda n, c: (xy_copy(15 - n).start(), c)[1], 0)

    level = jnp.full((1, TC), noise_ref[0], jnp.int32).astype(F32) / (NOISE_LEVELS - 1)
    sigma = jnp.exp(math.log(2.0) + level * (math.log(0.05) - math.log(2.0)))
    scale = 1.0 / jnp.sqrt(sigma * sigma + 0.25)

    def back_step(n, carry):
        back = jnp.zeros((CPAD, 2 * TC), F32)
        for a in range(3):
            start = pl.multiple_of((2 * n + 2 - a) * TC, TC)
            back = back + lax.dot_general(
                wcat[a], dzc[pl.ds(start, 2 * TC), :], (((1,), (1,)), ((), ())),
                preferred_element_type=F32,
            )
        for half in range(2):
            part = back[:, half * TC : (half + 1) * TC]
            bk32[2 * n + half, :CPAD, :] = part
            d32[pl.ds(2 * n + half, CR, stride=TR), :] = part[:CR] * scale
        return carry

    lax.fori_loop(0, TR // 2, back_step, 0)

    def igrad_step(n, carry):
        rows = d32[pl.ds(pl.multiple_of(n * 9 * TR, 16), 9 * TR), :]
        ig_v[pl.ds(n * 9, 9)] = rows.reshape(9, TR, TC).astype(BF16)
        return carry

    lax.fori_loop(0, CR // 9, igrad_step, 0)
    store = pltpu.make_async_copy(ig_v, igrad_hbm.at[0], out_sem.at[0])
    store.start()

    home = (reg * 4 + glob) * 2
    wanted = [(home + step + NGB) % NGB for step in (-1, 0, 1, 2, NGB // 2)]
    for i in range(TR):
        cond = bk32[i, CR : CR + BLK, :].astype(BF16).astype(F32)
        target = targets_ref[0, i]
        for n in range(5):
            mask = (target == wanted[n]).astype(F32)
            cmask[n * BLK : (n + 1) * BLK, i * TC : (i + 1) * TC] = (cond * mask).astype(BF16)
    loads[4].wait()
    glob_out[...] = jnp.dot(
        cmask[...], interp_v[...].reshape(TR * TC, TC), preferred_element_type=F32
    ).reshape(5, BLK, TC)
    glob_copies = []
    for n, (block, step) in enumerate(((0, -1), (3, 1), (4, 64))):
        copy = pltpu.make_async_remote_copy(
            glob_out.at[block], glob_recv.at[n], gl_ss.at[n], gl_rs.at[n],
            device_id=flat_dev(step), device_id_type=MESH,
        )
        copy.start()
        glob_copies.append(copy)

    lax.fori_loop(1, 16, lambda d, c: (xy_copy(d).wait_recv(), c)[1], 0)
    piece = acc[pl.ds(pl.multiple_of(q * PIECE, 8), PIECE), :]
    for d in range(1, 16):
        piece = piece + xrecv[d]
    zbuf[z] = piece

    def z_copy(d):
        return pltpu.make_async_remote_copy(
            zbuf.at[z], zbuf.at[z], z_ss.at[d], z_rs.at[d],
            device_id=z_dev(d), device_id_type=MESH,
        )

    def z_arrival(d):
        slot = (z - d + 8) % 8
        return pltpu.make_async_remote_copy(
            zbuf.at[slot], zbuf.at[slot], z_ss.at[d], z_rs.at[d],
            device_id=z_dev(d), device_id_type=MESH,
        )

    lax.fori_loop(1, 8, lambda d, c: (z_copy(d).start(), c)[1], 0)

    for copy in glob_copies:
        copy.wait_recv()
    own[0] = glob_out[1] + glob_recv[1] + glob_recv[2]
    own[1] = glob_out[2] + glob_recv[0]
    cpl_copy = pltpu.make_async_remote_copy(
        own, cplrecv, gl_ss.at[3], gl_rs.at[3], device_id=other, device_id_type=MESH
    )
    cpl_copy.start()

    lax.fori_loop(1, 8, lambda d, c: (z_arrival(d).wait_recv(), c)[1], 0)
    full = zbuf[0]
    for n in range(1, 8):
        full = full + zbuf[n]
    fbuf[:PIECE, :] = full * SCALE_NORM
    fbuf[PIECE:, :] = jnp.zeros((PIECE_B - PIECE, CH), F32)
    gbuf[core, q] = fbuf[...].astype(BF16)

    def ag_copy(d, slot):
        return pltpu.make_async_remote_copy(
            gbuf.at[core, slot], gbuf.at[core, slot], ag_ss.at[d], ag_rs.at[d],
            device_id=plane_dev(d), device_id_type=MESH,
        )

    def source(d):
        return ((x + 4 - d // 4) % 4) * 4 + (y + 4 - d % 4) % 4

    def fw_copy(d, half):
        slot = source(d)
        return pltpu.make_async_remote_copy(
            gbuf.at[half, slot], gbuf.at[half, slot], fw_ss.at[d], fw_rs.at[d],
            device_id=sibling, device_id_type=MESH,
        )

    lax.fori_loop(0, 15, lambda n, c: (ag_copy(15 - n, q).start(), c)[1], 0)
    fw_copy(0, core).start()

    cpl_copy.wait_recv()
    ggrad_ref[...] = (own[...] + cplrecv[...])[:, :CG, :]

    def arrive(d, carry):
        ag_copy(d, source(d)).wait_recv()
        fw_copy(d, core).start()
        return carry

    lax.fori_loop(1, 16, arrive, 0)
    lax.fori_loop(0, 16, lambda d, c: (fw_copy(d, 1 - core).wait_recv(), c)[1], 0)

    for h in range(2):
        for p in range(16):
            part = gbuf[h, p].astype(F32)
            for s in range(PIECE // 8):
                row = p * PIECE + s * 8
                if row >= ROWS_HALF:
                    continue
                k, c = row // HALF, row % HALF + h * HALF
                keep = min(8, CIN - c)
                wgrad_ref[k, c : c + keep, :] = part[s * 8 : s * 8 + keep]
                if h == 1 and k == 0 and c <= CIN < c + 8:
                    bgrad_ref[...] = part[s * 8 + CIN - c : s * 8 + CIN - c + 1]

    store.wait()
    for copy in halo + core_copies + glob_copies + [cpl_copy]:
        copy.wait_send()
    lax.fori_loop(1, 16, lambda d, c: (xy_copy(d).wait_send(), c)[1], 0)
    lax.fori_loop(1, 8, lambda d, c: (z_copy(d).wait_send(), c)[1], 0)
    lax.fori_loop(1, 16, lambda d, c: (ag_copy(d, q).wait_send(), c)[1], 0)
    lax.fori_loop(0, 16, lambda d, c: (fw_copy(d, core).wait_send(), c)[1], 0)


def body(saved_input, pre_act, cotangent, conv_weight, interp, targets, noise_index):
    vmem = pl.BlockSpec(memory_space=pltpu.VMEM)
    smem = pl.BlockSpec(memory_space=pltpu.SMEM)
    any_ = pl.BlockSpec(memory_space=pl.ANY)
    dma = pltpu.SemaphoreType.DMA
    igrad, wgrad, bgrad, ggrad = pl.pallas_call(
        kernel,
        out_shape=(
            jax.ShapeDtypeStruct((1, CR, TR, TC), BF16),
            jax.ShapeDtypeStruct((9, CIN, CH), F32),
            jax.ShapeDtypeStruct((1, CH), F32),
            jax.ShapeDtypeStruct((2, CG, TC), F32),
        ),
        in_specs=[any_] * 5 + [smem] * 2,
        out_specs=(any_, vmem, vmem, vmem),
        scratch_shapes=[
            pltpu.VMEM((CIN, TR, TC), BF16),
            pltpu.VMEM((CH, TR, TC), BF16),
            pltpu.VMEM((CH, TR, TC), BF16),
            pltpu.VMEM((9, CIN, CH), BF16),
            pltpu.VMEM((TR, TC, TC), BF16),
            pltpu.VMEM((CH * TR, TC), F32),
            pltpu.VMEM((CPAD * TR, TC), F32),
            pltpu.VMEM((TR + 2, PITCH, CH), F32),
            pltpu.VMEM(((TR + 2) * TC, 3 * CH), BF16),
            pltpu.VMEM((CPAD, TR * TC), BF16),
            pltpu.VMEM((3, CPAD, 3 * CH), BF16),
            pltpu.VMEM((2, TR, CH), F32),
            pltpu.VMEM((2, TR, CH), F32),
            pltpu.VMEM((2, 2, 8, CH), F32),
            pltpu.VMEM((2, ROWS_HALF, CH), F32),
            pltpu.VMEM((ROWS_HALF, CH), F32),
            pltpu.VMEM((ROWS_ALL, CH), F32),
            pltpu.VMEM((16, PIECE, CH), F32),
            pltpu.VMEM((8, PIECE, CH), F32),
            pltpu.VMEM((PIECE_B, CH), F32),
            pltpu.VMEM((2, 16, PIECE_B, CH), BF16),
            pltpu.VMEM((TR, CPAD + 8, TC), F32),
            pltpu.VMEM((5 * BLK, TR * TC), BF16),
            pltpu.VMEM((5, BLK, TC), F32),
            pltpu.VMEM((3, BLK, TC), F32),
            pltpu.VMEM((2, BLK, TC), F32),
            pltpu.VMEM((2, BLK, TC), F32),
            pltpu.VMEM((CR, TR, TC), BF16),
            dma((5,)),
            dma((8,)),
            dma((8,)),
            dma((3,)),
            dma((3,)),
            dma((16,)),
            dma((16,)),
            dma((8,)),
            dma((8,)),
            dma((16,)),
            dma((16,)),
            dma((16,)),
            dma((16,)),
            dma((4,)),
            dma((4,)),
            dma((1,)),
        ],
        compiler_params=pltpu.CompilerParams(
            collective_id=0, has_side_effects=True, vmem_limit_bytes=40 << 20
        ),
        cost_estimate=pl.CostEstimate(
            flops=2 * 2 * CIN * 9 * CH * TR * TC, bytes_accessed=4 << 20, transcendentals=CH * TR * TC
        ),
    )(saved_input, pre_act, cotangent, conv_weight, interp, targets, noise_index)
    return igrad, wgrad, bgrad.reshape(CH), ggrad


def solution(mesh):
    in_specs = (
        P("cpl", None, "reg", "glob"),
        P("cpl", None, "reg", "glob"),
        P("cpl", None, "reg", "glob"),
        P(),
        P("glob", "reg", None, None),
        P("glob", "reg"),
        P("cpl"),
    )
    out_specs = (P("cpl", None, "reg", "glob"), P(), P(), P(("reg", "glob"), None, None))
    return jax.shard_map(body, mesh=mesh, in_specs=in_specs, out_specs=out_specs, check_vma=False)
```

time: 1480 us -> 54.1 us (0.04)
  waiting for transfers between devices: 1320 us -> 0 us
  blocking collectives: 82.6 us -> 0 us
  Pallas kernels: 0 us -> 44.4 us
  local copies, waits for them, and re-layouts: 24.9 us -> 8.04 us
    unnamed x4 -> x0, waiting for transfers between devices: 1020 us -> none
    psum x2 -> x0, waiting for transfers between devices: 295 us -> none  [the longest x1 260 us: body(): lax.psum((weight_term, jnp.sum(dz32, axis=(1, 2))), ('reg', 'glob', 'cpl'))]
    psum x1 -> x0, blocking collectives: 82.6 us -> none  [body(): lax.psum((weight_term, jnp.sum(dz32, axis=(1, 2))), ('reg', 'glob', 'cpl'))]
    pallas_call x0 -> x1, Pallas kernels: none -> 44.4 us  [body(): pl.pallas_call(kernel, out_shape=(jax.ShapeDtypeStruct((1, CR, TR, TC), B...]
  transfers between devices with their start and end apart: 7 -> 0, of which waited for: 5 -> 0; matrix products, arithmetic and copies ran while one was open for 1% -> 0% of each run, Pallas kernels for 0% -> 0%
where the time goes in v1:
time: 54.1 us; the launch traced here: 53.8 us
  Pallas kernels  44.4 us (82%)
  local copies, waits for them, and re-layouts  8.04 us (15%)
  between operations  1.33 us (2%)
    pallas_call x1, Pallas kernels, body(): pl.pallas_call(kernel, out_shape=(jax.ShapeDtypeStruct((1, CR, TR, TC), B...  44.4 us
    unnamed x16, local copies, waits for them, and re-layouts  8.04 us

profile of v1, /device:TPU:1, one launch (start us, length us, event | category | flops | bytes accessed | tf_op | source)
XLA Modules:
  0.0 53.8 jit_solution(6196118962933631435)
XLA Ops:
  0.6 0.0 copy-start.5
  1.3 0.0 copy-done.5
  1.3 0.0 copy-start
  1.3 1.1 %copy-done = bf16[1,172,16,128]{3,2,1,0:T(8,128)(2,1)S(1)} copy-done((bf16[1,172,16,128]{3,2,1,0:T(8,128)(2,1)S(1)}, bf16[1,172,16,128]{3,2,1,0:T(8,128)(2,1)}, u32[]{:S(2)}) %copy-start) | copy-done | bytes 704536
  2.4 0.0 copy-start.1
  2.4 1.0 %copy-done.1 = bf16[1,128,16,128]{3,2,1,0:T(8,128)(2,1)S(1)} copy-done((bf16[1,128,16,128]{3,2,1,0:T(8,128)(2,1)S(1)}, bf16[1,128,16,128]{3,2,1,0:T(8,128)(2,1)}, u32[]{:S(2)}) %copy-start.1) | copy-done | bytes 524312
  3.5 0.0 copy-start.2
  3.5 1.0 %copy-done.2 = bf16[1,128,16,128]{3,2,1,0:T(8,128)(2,1)S(1)} copy-done((bf16[1,128,16,128]{3,2,1,0:T(8,128)(2,1)S(1)}, bf16[1,128,16,128]{3,2,1,0:T(8,128)(2,1)}, u32[]{:S(2)}) %copy-start.2) | copy-done | bytes 524312
  4.5 0.0 copy-start.3
  4.5 1.0 %copy-done.3 = bf16[1,16,128,128]{3,2,1,0:T(8,128)(2,1)S(1)} copy-done((bf16[1,16,128,128]{3,2,1,0:T(8,128)(2,1)S(1)}, bf16[1,16,128,128]{3,2,1,0:T(8,128)(2,1)}, u32[]{:S(2)}) %copy-start.3) | copy-done | bytes 524312
  5.5 0.0 copy-start.4
  5.5 1.0 %copy-done.4 = bf16[9,172,128]{2,1,0:T(8,128)(2,1)S(1)} copy-done((bf16[9,172,128]{2,1,0:T(8,128)(2,1)S(1)}, bf16[9,172,128]{2,1,0:T(8,128)(2,1)}, u32[]{:S(2)}) %copy-start.4) | copy-done | bytes 396312
  6.5 44.4 %shard_map.102 = (bf16[1,99,16,128]{3,2,1,0:T(8,128)(2,1)S(1)}, f32[9,172,128]{2,1,0:T(8,128)S(1)}, f32[1,128]{1,0:T(1,128)S(1)}, f32[2,73,128]{2,1,0:T(8,128)S(1)}) custom-call(bf16[1,172,16,128]{3,2,1,0:T(8,128)(2,1)S(1)} %copy-done, bf16[1,128,16,128]{3,2,1,0:T(8,128)(2,1)S(1)} %copy-done.1, bf16[1,128,16,128]{3,2,1,0:T(8,128)(2,1)S(1)} %copy-done.2, ...), custom_call_target="tpu_custom_call" | custom-call | flops 1623195648 | bytes 4194304 | tf_op jit(solution)/shard_map/pallas_call | solution.py:376
  50.9 0.7 %copy.11 = f32[2,73,128]{2,0,1:T(2,128)} copy(f32[2,73,128]{2,1,0:T(8,128)S(1)} %get-tuple-element.15) | data formatting | bytes 149504
  51.6 0.7 %copy.16 = bf16[1,99,16,128]{3,2,1,0:T(8,128)(2,1)} copy(bf16[1,99,16,128]{3,2,1,0:T(8,128)(2,1)S(1)} %get-tuple-element.20) | data formatting | bytes 811008
  52.4 0.9 %copy.17 = f32[9,172,128]{2,1,0:T(8,128)} copy(f32[9,172,128]{2,1,0:T(8,128)S(1)} %get-tuple-element.21) | data formatting | bytes 1585152
  53.2 0.5 copy.18
Async XLA Ops:
  0.6 0.7 %copy-start.5 = (s32[1,16]{1,0:T(1,128)S(1)}, s32[1,16]{1,0:T(1,128)}, u32[]{:S(2)}) copy-start(s32[1,16]{1,0:T(1,128)} %targets_ref.1) | copy-start | bytes 196
  1.3 1.1 %copy-start = (bf16[1,172,16,128]{3,2,1,0:T(8,128)(2,1)S(1)}, bf16[1,172,16,128]{3,2,1,0:T(8,128)(2,1)}, u32[]{:S(2)}) copy-start(bf16[1,172,16,128]{3,2,1,0:T(8,128)(2,1)} %saved_hbm.1) | copy-start | bytes 2113540
  2.4 1.0 %copy-start.1 = (bf16[1,128,16,128]{3,2,1,0:T(8,128)(2,1)S(1)}, bf16[1,128,16,128]{3,2,1,0:T(8,128)(2,1)}, u32[]{:S(2)}) copy-start(bf16[1,128,16,128]{3,2,1,0:T(8,128)(2,1)} %pre_hbm.1) | copy-start | bytes 1572868
  3.5 1.0 %copy-start.2 = (bf16[1,128,16,128]{3,2,1,0:T(8,128)(2,1)S(1)}, bf16[1,128,16,128]{3,2,1,0:T(8,128)(2,1)}, u32[]{:S(2)}) copy-start(bf16[1,128,16,128]{3,2,1,0:T(8,128)(2,1)} %cot_hbm.1) | copy-start | bytes 1572868
  4.5 1.0 %copy-start.3 = (bf16[1,16,128,128]{3,2,1,0:T(8,128)(2,1)S(1)}, bf16[1,16,128,128]{3,2,1,0:T(8,128)(2,1)}, u32[]{:S(2)}) copy-start(bf16[1,16,128,128]{3,2,1,0:T(8,128)(2,1)} %interp_hbm.1) | copy-start | bytes 1572868
  5.5 1.0 %copy-start.4 = (bf16[9,172,128]{2,1,0:T(8,128)(2,1)S(1)}, bf16[9,172,128]{2,1,0:T(8,128)(2,1)}, u32[]{:S(2)}) copy-start(bf16[9,172,128]{2,1,0:T(8,128)(2,1)} %w_hbm.1) | copy-start | bytes 1188868

commit v2 on v1

v2 whole, which is shorter than its diff:
```python
import math

import jax
import jax.numpy as jnp
from jax import lax
from jax.experimental import pallas as pl
from jax.experimental.pallas import tpu as pltpu
from jax.sharding import PartitionSpec as P

CH = 128
CR = 99
CG = 73
CIN = 172
CPAD = 176
HALF = 88
TR = 16
TC = 128
NGB = 256
NOISE_LEVELS = 18
PIECE = 64
ROWS_HALF = 9 * HALF
ROWS_PAD = 800
ROWS_ALL = 16 * PIECE
TOP = 8
PITCH = TOP + TC + 8
BLK = 80
SCALE_NORM = 1.0 / math.sqrt(512 * 512 * 2)
MESH = pl.DeviceIdType.MESH
F32 = jnp.float32
BF16 = jnp.bfloat16


def kernel(
    saved_hbm, pre_hbm, cot_hbm, w_hbm, interp_hbm, targets_hbm, noise_ref,
    ig_v, gbuf, ggrad_ref,
    saved_v, pre_v, cot_v, w_v, interp_v, targets_ref,
    d32, s32, p32, dzc, smat, wcat, colbuf, colrecv, corner,
    pick, edge, lpad, extra,
    awh, crecv, acc, xrecv, zbuf,
    bk32, cmask, glob_out, glob_recv, own, cplrecv,
    in_sem, halo_ss, halo_rs, core_ss, core_rs, xy_ss, xy_rs, z_ss, z_rs,
    ag_ss, ag_rs, fw_ss, fw_rs, gl_ss, gl_rs,
):
    reg = lax.axis_index("reg")
    glob = lax.axis_index("glob")
    cpl = lax.axis_index("cpl")
    z = reg // 4
    x_lo = (reg // 2) % 2
    core = reg % 2
    x = cpl * 2 + x_lo
    y = glob
    q = x * 4 + y

    def at(x_, y_, z_, core_):
        return {"reg": z_ * 4 + (x_ % 2) * 2 + core_, "glob": y_, "cpl": x_ // 2}

    def plane(d):
        return (x + d // 4) % 4, (y + d % 4) % 4

    def plane_dev(d):
        px, py = plane(d)
        return at(px, py, z, core)

    def z_dev(d):
        return at(x, y, (z + d) % 8, core)

    def halo_dev(dr, dg):
        return {"reg": (reg + dr + 32) % 32, "glob": (glob + dg + 4) % 4, "cpl": cpl}

    def flat_dev(step):
        flat = (reg * 4 + glob + step + 128) % 128
        return {"reg": flat // 4, "glob": flat % 4, "cpl": cpl}

    sibling = at(x, y, z, 1 - core)
    other = {"reg": reg, "glob": glob, "cpl": 1 - cpl}

    loads = [
        pltpu.make_async_copy(src, dst, in_sem.at[n])
        for n, (src, dst) in enumerate((
            (pre_hbm.at[0], pre_v),
            (cot_hbm.at[0], cot_v),
            (saved_hbm.at[0], saved_v),
            (w_hbm, w_v),
            (interp_hbm.at[0], interp_v),
            (targets_hbm, targets_ref),
        ))
    ]
    for load in loads:
        load.start()
    pend = {n: load.wait for n, load in enumerate(loads)}

    barrier = pltpu.get_barrier_semaphore()

    def greet(device):
        pl.semaphore_signal(barrier, inc=1, device_id=device, device_id_type=MESH)

    halo_steps = [(dr, dg) for dr in (-1, 0, 1) for dg in (-1, 0, 1) if dr or dg]
    for dr, dg in halo_steps:
        greet(halo_dev(dr, dg))
    for step in (-1, 1, 64):
        greet(flat_dev(step))
    greet(other)
    greet(sibling)
    lax.fori_loop(1, 16, lambda d, c: (greet(plane_dev(d)), c)[1], 0)
    lax.fori_loop(1, 8, lambda d, c: (greet(z_dev(d)), c)[1], 0)

    s32[CIN * TR :, :] = jnp.zeros((CPAD * TR - CIN * TR, TC), F32)
    wcat[:, CPAD - 16 :, :] = jnp.zeros((3, 16, 3 * CH), BF16)
    acc[ROWS_PAD:, :] = jnp.zeros((ROWS_ALL - ROWS_PAD, CH), BF16)
    awh[:, ROWS_HALF:, :] = jnp.zeros((2, ROWS_PAD - ROWS_HALF, CH), F32)
    crecv[ROWS_HALF:, :] = jnp.zeros((ROWS_PAD - ROWS_HALF, CH), F32)
    for i in range(TR):
        p32[i + 1, :TOP, :] = jnp.zeros((TOP, CH), F32)
        p32[i + 1, TOP + TC :, :] = jnp.zeros((8, CH), F32)
    lpad[...] = jnp.zeros((2, 24, CH), F32)
    extra[...] = jnp.zeros((3, TC, 3 * CH), BF16)
    bk32[:, CPAD:, :] = jnp.zeros((TR, 8, TC), F32)

    pend.pop(0)()
    pend.pop(1)()

    def silu_step(n, carry):
        pre = pre_v[pl.ds(n * 8, 8)].astype(F32)
        cot = cot_v[pl.ds(n * 8, 8)].astype(F32)
        sig = 0.5 * jnp.tanh(0.5 * pre) + 0.5
        dz = cot * sig * (1.0 + pre * (1.0 - sig))
        d32[pl.ds(pl.multiple_of(n * 8 * TR, 128), 8 * TR), :] = dz.reshape(8 * TR, TC)
        return carry

    lax.fori_loop(0, CH // 8, silu_step, 0)

    def turn(i):
        tile = jnp.transpose(d32[pl.ds(i, CH, stride=TR), :], (1, 0))
        p32[i + 1, TOP : TOP + TC, :] = tile
        colbuf[0, i : i + 1, :] = tile[:1]
        colbuf[1, i : i + 1, :] = tile[TC - 1 :]
        return tile

    total = jnp.zeros((TC, CH), F32)
    for i in range(TR):
        total = total + turn(i)
    bias = jnp.sum(total, axis=0, keepdims=True)

    pl.semaphore_wait(barrier, 8 + 3 + 1 + 1 + 15 + 7)

    for dr, dg in halo_steps:
        row = TR if dr > 0 else 1
        if dg == 0:
            kind = 0
            src = p32.at[row, pl.ds(TOP, TC)]
            dst = p32.at[0 if dr > 0 else TR + 1, pl.ds(TOP, TC)]
        elif dr == 0:
            kind = 1
            src = colbuf.at[1 if dg > 0 else 0]
            dst = colrecv.at[0 if dg > 0 else 1]
        else:
            kind = 2
            src = p32.at[row, pl.ds(TOP + TC - 8 if dg > 0 else TOP, 8)]
            dst = corner.at[0 if dr > 0 else 1, 0 if dg > 0 else 1]
        pltpu.make_async_remote_copy(
            src, dst, halo_ss.at[kind], halo_rs.at[kind],
            device_id=halo_dev(dr, dg), device_id_type=MESH,
        ).start()

    def bulk(ref, sem):
        return pltpu.make_async_copy(ref, ref, sem).wait

    halo_bulk = (d32.at[pl.ds(0, 2 * TC)], colrecv, corner)
    for kind in range(3):
        pend["halo_s", kind] = bulk(halo_bulk[kind], halo_ss.at[kind])
        pend["halo", kind] = bulk(halo_bulk[kind], halo_rs.at[kind])

    pend.pop(2)()

    def saved_step(n, carry):
        part = saved_v[pl.ds(n * 4, 4)].astype(F32)
        s32[pl.ds(pl.multiple_of(n * 4 * TR, 64), 4 * TR), :] = part.reshape(4 * TR, TC)
        return carry

    lax.fori_loop(0, CIN // 4, saved_step, 0)
    for i in range(TR):
        smat[:, i * TC : (i + 1) * TC] = s32[pl.ds(i, CPAD, stride=TR), :].astype(BF16)

    def shift_rows(i):
        for bi in range(3):
            dzc[pl.ds(pl.multiple_of(i * TC, TC), TC), bi * CH : (bi + 1) * CH] = p32[
                i, TOP + 1 - bi : TOP + 1 - bi + TC, :
            ].astype(BF16)

    lax.fori_loop(1, TR + 1, lambda i, c: (shift_rows(i), c)[1], 0)
    border = jnp.zeros((TC, 3 * CH), BF16)
    dzc[:TC, :] = border
    dzc[(TR + 1) * TC :, :] = border
    for a in range(3):
        term = jnp.dot(
            smat[...], dzc[(2 - a) * TC : (2 - a) * TC + TR * TC, :],
            preferred_element_type=F32,
        )
        for bi in range(3):
            k = 3 * a + bi
            for h in range(2):
                awh[h, k * HALF : (k + 1) * HALF, :] = term[
                    h * HALF : (h + 1) * HALF, bi * CH : (bi + 1) * CH
                ]
    awh[1, CIN - HALF : CIN - HALF + 1, :] = bias

    at_row = lax.broadcasted_iota(jnp.int32, (TC, TC), 0)
    at_lane = lax.broadcasted_iota(jnp.int32, (TC, TC), 1)
    for i in range(TR):
        first = (at_row == 0) & (at_lane == i)
        last = (at_row == TC - 1) & (at_lane == TR + i)
        pick[i * TC : (i + 1) * TC, :] = jnp.where(first | last, 1.0, 0.0).astype(BF16)
    edge[...] = jnp.dot(smat[...], pick[...], preferred_element_type=F32).astype(BF16)

    pend.pop(3)()
    for a in range(3):
        for bi in range(3):
            wcat[a, :CIN, bi * CH : (bi + 1) * CH] = w_v[3 * a + bi]

    for kind in range(3):
        pend.pop(("halo", kind))()
    up = (reg > 0).astype(F32)
    down = (reg < 31).astype(F32)
    left = (glob > 0).astype(F32)
    right = (glob < 3).astype(F32)
    p32[0, TOP : TOP + TC, :] = p32[0, TOP : TOP + TC, :] * up
    p32[TR + 1, TOP : TOP + TC, :] = p32[TR + 1, TOP : TOP + TC, :] * down
    lpad[0, 1 : TR + 1, :] = colrecv[0] * left
    lpad[1, 1 : TR + 1, :] = colrecv[1] * right
    for i in range(TR):
        p32[i + 1, TOP - 1 : TOP, :] = lpad[0, i + 1 : i + 2, :]
        p32[i + 1, TOP + TC : TOP + TC + 1, :] = lpad[1, i + 1 : i + 2, :]
    p32[0, TOP - 1 : TOP, :] = corner[0, 0, 7:8, :] * (up * left)
    p32[0, TOP + TC : TOP + TC + 1, :] = corner[0, 1, 0:1, :] * (up * right)
    p32[TR + 1, TOP - 1 : TOP, :] = corner[1, 0, 7:8, :] * (down * left)
    p32[TR + 1, TOP + TC : TOP + TC + 1, :] = corner[1, 1, 0:1, :] * (down * right)
    shift_rows(0)
    shift_rows(TR + 1)
    for a in range(3):
        extra[a, :TR, 2 * CH :] = lpad[0, 2 - a : 2 - a + TR, :].astype(BF16)
        extra[a, TR : 2 * TR, :CH] = lpad[1, 2 - a : 2 - a + TR, :].astype(BF16)

    for a in range(3):
        term = jnp.dot(edge[...], extra[a], preferred_element_type=F32)
        if a == 0:
            term = term + jnp.dot(
                smat[:, (TR - 1) * TC :], dzc[(TR + 1) * TC :, :], preferred_element_type=F32
            )
        if a == 2:
            term = term + jnp.dot(smat[:, :TC], dzc[:TC, :], preferred_element_type=F32)
        for bi in range(3):
            k = 3 * a + bi
            for h in range(2):
                rows = slice(k * HALF, (k + 1) * HALF)
                awh[h, rows, :] = awh[h, rows, :] + term[
                    h * HALF : (h + 1) * HALF, bi * CH : (bi + 1) * CH
                ]
        if a == 0:
            awh[1, CIN - HALF : CIN - HALF + 1, :] = bias
        rows = pl.ds(3 * a * HALF, 3 * HALF)
        pltpu.make_async_remote_copy(
            awh.at[1 - core, rows], crecv.at[rows], core_ss, core_rs,
            device_id=sibling, device_id_type=MESH,
        ).start()
    pend["core_s"] = bulk(crecv.at[pl.ds(0, ROWS_HALF)], core_ss)
    pend["core"] = bulk(crecv.at[pl.ds(0, ROWS_HALF)], core_rs)
    lax.fori_loop(1, TR + 1, lambda i, c: (shift_rows(i), c)[1], 0)
    pend.pop("core")()
    acc[:ROWS_PAD, :] = (awh[core] + crecv[...]).astype(BF16)
    def xy_start(n, carry):
        d = 15 - n
        px, py = plane(d)
        pltpu.make_async_remote_copy(
            acc.at[pl.ds(pl.multiple_of((px * 4 + py) * PIECE, PIECE), PIECE)],
            xrecv.at[d], xy_ss, xy_rs,
            device_id=at(px, py, z, core), device_id_type=MESH,
        ).start()
        return carry

    lax.fori_loop(0, 15, xy_start, 0)
    pend["xy_s"] = bulk(xrecv.at[pl.ds(1, 15)], xy_ss)
    pend["xy"] = bulk(xrecv.at[pl.ds(1, 15)], xy_rs)

    level = jnp.full((1, TC), noise_ref[0], jnp.int32).astype(F32) / (NOISE_LEVELS - 1)
    sigma = jnp.exp(math.log(2.0) + level * (math.log(0.05) - math.log(2.0)))
    scale = 1.0 / jnp.sqrt(sigma * sigma + 0.25)

    def back_step(n, carry):
        back = jnp.zeros((CPAD, 2 * TC), F32)
        for a in range(3):
            start = pl.multiple_of((2 * n + 2 - a) * TC, TC)
            back = back + lax.dot_general(
                wcat[a], dzc[pl.ds(start, 2 * TC), :], (((1,), (1,)), ((), ())),
                preferred_element_type=F32,
            )
        for half in range(2):
            part = back[:, half * TC : (half + 1) * TC]
            bk32[2 * n + half, :CPAD, :] = part
            d32[pl.ds(2 * n + half, CR, stride=TR), :] = part[:CR] * scale
        return carry

    lax.fori_loop(0, TR // 2, back_step, 0)

    def igrad_step(n, carry):
        rows = d32[pl.ds(pl.multiple_of(n * 9 * TR, 16), 9 * TR), :]
        ig_v[pl.ds(n * 9, 9)] = rows.reshape(9, TR, TC).astype(BF16)
        return carry

    lax.fori_loop(0, CR // 9, igrad_step, 0)
    pend.pop(5)()
    home = (reg * 4 + glob) * 2
    wanted = [(home + step + NGB) % NGB for step in (-1, 0, 1, 2, NGB // 2)]
    for i in range(TR):
        cond = bk32[i, CR : CR + BLK, :].astype(BF16).astype(F32)
        target = targets_ref[0, i]
        for n in range(5):
            mask = (target == wanted[n]).astype(F32)
            cmask[n * BLK : (n + 1) * BLK, i * TC : (i + 1) * TC] = (cond * mask).astype(BF16)
    pend.pop(4)()
    glob_out[...] = jnp.dot(
        cmask[...], interp_v[...].reshape(TR * TC, TC), preferred_element_type=F32
    ).reshape(5, BLK, TC)
    for n, (block, step) in enumerate(((0, -1), (3, 1), (4, 64))):
        pltpu.make_async_remote_copy(
            glob_out.at[block], glob_recv.at[n], gl_ss.at[0], gl_rs.at[0],
            device_id=flat_dev(step), device_id_type=MESH,
        ).start()
    pend["glob_s"] = bulk(glob_recv, gl_ss.at[0])
    pend["glob"] = bulk(glob_recv, gl_rs.at[0])
    pend.pop("xy")()
    piece = acc[pl.ds(pl.multiple_of(q * PIECE, PIECE), PIECE), :].astype(F32)
    for d in range(1, 16):
        piece = piece + xrecv[d].astype(F32)
    zbuf[z] = piece.astype(BF16)

    def z_start(d, carry):
        pltpu.make_async_remote_copy(
            zbuf.at[z], zbuf.at[z], z_ss, z_rs, device_id=z_dev(d), device_id_type=MESH
        ).start()
        return carry

    lax.fori_loop(1, 8, z_start, 0)
    pend["z_s"] = bulk(zbuf.at[pl.ds(0, 7)], z_ss)
    pend["z"] = bulk(zbuf.at[pl.ds(0, 7)], z_rs)

    pend.pop("glob")()
    own[0] = glob_out[1] + glob_recv[1] + glob_recv[2]
    own[1] = glob_out[2] + glob_recv[0]
    cpl_copy = pltpu.make_async_remote_copy(
        own, cplrecv, gl_ss.at[1], gl_rs.at[1], device_id=other, device_id_type=MESH
    )
    cpl_copy.start()
    pend["cpl_s"] = cpl_copy.wait_send
    pend["cpl"] = cpl_copy.wait_recv

    pend.pop("z")()
    full = zbuf[0].astype(F32)
    for n in range(1, 8):
        full = full + zbuf[n].astype(F32)
    gbuf[core, q] = (full * SCALE_NORM).astype(BF16)

    def ag_start(n, carry):
        d = 15 - n
        pltpu.make_async_remote_copy(
            gbuf.at[core, q], gbuf.at[core, q], ag_ss, ag_rs.at[d // 4],
            device_id=plane_dev(d), device_id_type=MESH,
        ).start()
        return carry

    lax.fori_loop(0, 15, ag_start, 0)
    pend["ag_s"] = bulk(gbuf.at[0, pl.ds(0, 15)], ag_ss)

    pend.pop("cpl")()
    ggrad_ref[...] = own[...] + cplrecv[...]

    for dx in (0, 1, 3, 2):
        count = 3 if dx == 0 else 4
        bulk(gbuf.at[0, pl.ds(0, count)], ag_rs.at[dx])()
        column = gbuf.at[core, pl.ds(lax.rem(x + 4 - dx, 4) * 4, 4)]
        pltpu.make_async_remote_copy(
            column, column, fw_ss, fw_rs, device_id=sibling, device_id_type=MESH
        ).start()
    pend["fw_s"] = bulk(gbuf.at[0], fw_ss)
    bulk(gbuf.at[0], fw_rs)()
    for wait in pend.values():
        wait()


def finish(ig_v, gbuf, gg_v, igrad_hbm, wgrad_hbm, bgrad_hbm, ggrad_hbm, w32, b32, g32, sem):
    first = pltpu.make_async_copy(ig_v, igrad_hbm.at[0], sem.at[0])
    first.start()
    for n in range(2):
        g32[:, n : n + 1, :] = gg_v[n, :CG, :].reshape(CG, 1, TC)
    second = pltpu.make_async_copy(g32, ggrad_hbm, sem.at[1])
    second.start()
    for h in range(2):
        for p in range(16):
            part = gbuf[h, p].astype(F32)
            for s in range(PIECE // 8):
                row = p * PIECE + s * 8
                if row >= ROWS_HALF:
                    continue
                k, c = row // HALF, row % HALF + h * HALF
                keep = min(8, CIN - c)
                w32[k, c : c + keep, :] = part[s * 8 : s * 8 + keep]
                if h == 1 and k == 0 and c <= CIN < c + 8:
                    b32[...] = part[s * 8 + CIN - c]

    third = pltpu.make_async_copy(w32, wgrad_hbm, sem.at[2])
    third.start()
    fourth = pltpu.make_async_copy(b32, bgrad_hbm, sem.at[3])
    fourth.start()
    for copy in (first, second, third, fourth):
        copy.wait()


def body(saved_input, pre_act, cotangent, conv_weight, interp, targets, noise_index):
    vmem = pl.BlockSpec(memory_space=pltpu.VMEM)
    smem = pl.BlockSpec(memory_space=pltpu.SMEM)
    hbm = pl.BlockSpec(memory_space=pltpu.HBM)
    dma = pltpu.SemaphoreType.DMA
    pinned = [
        pltpu.with_memory_space_constraint(v, pltpu.HBM)
        for v in (saved_input, pre_act, cotangent, conv_weight, interp, targets)
    ]
    parts = pl.pallas_call(
        kernel,
        out_shape=(
            jax.ShapeDtypeStruct((CR, TR, TC), BF16),
            jax.ShapeDtypeStruct((2, 16, PIECE, CH), BF16),
            jax.ShapeDtypeStruct((2, BLK, TC), F32),
        ),
        in_specs=[hbm] * 6 + [smem],
        out_specs=(vmem, vmem, vmem),
        scratch_shapes=[
            pltpu.VMEM((CIN, TR, TC), BF16),
            pltpu.VMEM((CH, TR, TC), BF16),
            pltpu.VMEM((CH, TR, TC), BF16),
            pltpu.VMEM((9, CIN, CH), BF16),
            pltpu.VMEM((TR, TC, TC), BF16),
            pltpu.SMEM((1, TR), jnp.int32),
            pltpu.VMEM((CH * TR, TC), F32),
            pltpu.VMEM((CPAD * TR, TC), F32),
            pltpu.VMEM((TR + 2, PITCH, CH), F32),
            pltpu.VMEM(((TR + 2) * TC, 3 * CH), BF16),
            pltpu.VMEM((CPAD, TR * TC), BF16),
            pltpu.VMEM((3, CPAD, 3 * CH), BF16),
            pltpu.VMEM((2, TR, CH), F32),
            pltpu.VMEM((2, TR, CH), F32),
            pltpu.VMEM((2, 2, 8, CH), F32),
            pltpu.VMEM((TR * TC, TC), BF16),
            pltpu.VMEM((CPAD, TC), BF16),
            pltpu.VMEM((2, 24, CH), F32),
            pltpu.VMEM((3, TC, 3 * CH), BF16),
            pltpu.VMEM((2, ROWS_PAD, CH), F32),
            pltpu.VMEM((ROWS_PAD, CH), F32),
            pltpu.VMEM((ROWS_ALL, CH), BF16),
            pltpu.VMEM((16, PIECE, CH), BF16),
            pltpu.VMEM((8, PIECE, CH), BF16),
            pltpu.VMEM((TR, CPAD + 8, TC), F32),
            pltpu.VMEM((5 * BLK, TR * TC), BF16),
            pltpu.VMEM((5, BLK, TC), F32),
            pltpu.VMEM((3, BLK, TC), F32),
            pltpu.VMEM((2, BLK, TC), F32),
            pltpu.VMEM((2, BLK, TC), F32),
            dma((6,)),
            dma((3,)),
            dma((3,)),
            dma,
            dma,
            dma,
            dma,
            dma,
            dma,
            dma,
            dma((4,)),
            dma,
            dma,
            dma((2,)),
            dma((2,)),
        ],
        compiler_params=pltpu.CompilerParams(
            collective_id=0, has_side_effects=True, vmem_limit_bytes=40 << 20
        ),
        cost_estimate=pl.CostEstimate(
            flops=2 * 2 * CIN * 9 * CH * TR * TC, bytes_accessed=4 << 20, transcendentals=CH * TR * TC
        ),
    )(*pinned, noise_index)
    igrad, wgrad, bgrad, ggrad = pl.pallas_call(
        finish,
        out_shape=(
            pltpu.HBM((1, CR, TR, TC), BF16),
            pltpu.HBM((9, CIN, CH), F32),
            pltpu.HBM((CH,), F32),
            pltpu.HBM((CG, 2, TC), F32),
        ),
        in_specs=[vmem] * 3,
        out_specs=(hbm, hbm, hbm, hbm),
        scratch_shapes=[
            pltpu.VMEM((9, CIN, CH), F32),
            pltpu.VMEM((CH,), F32),
            pltpu.VMEM((CG, 2, TC), F32),
            dma((4,)),
        ],
        compiler_params=pltpu.CompilerParams(vmem_limit_bytes=16 << 20),
    )(*parts)
    return igrad, wgrad, bgrad, jnp.transpose(ggrad, (1, 0, 2))


def solution(mesh):
    in_specs = (
        P("cpl", None, "reg", "glob"),
        P("cpl", None, "reg", "glob"),
        P("cpl", None, "reg", "glob"),
        P(),
        P("glob", "reg", None, None),
        P("glob", "reg"),
        P("cpl"),
    )
    out_specs = (P("cpl", None, "reg", "glob"), P(), P(), P(("reg", "glob"), None, None))
    return jax.shard_map(body, mesh=mesh, in_specs=in_specs, out_specs=out_specs, check_vma=False)
```

time: 54.1 us -> 39.6 us (0.73)
  local copies, waits for them, and re-layouts: 8.04 us -> 0 us
  Pallas kernels: 44.4 us -> 38.2 us
    unnamed x16 -> x0, local copies, waits for them, and re-layouts: 8.04 us -> none
    pallas_call x1 -> x2, Pallas kernels: 44.4 us -> 38.2 us  [the longest x1 37.1 us: body(): pl.pallas_call(kernel, out_shape=(jax.ShapeDtypeStruct((CR, TR, TC), BF16...]
where the time goes in v2:
time: 39.6 us; the launch traced here: 39.5 us
  Pallas kernels  38.2 us (96%)
  between operations  1.29 us (3%)
    pallas_call x1, Pallas kernels, body(): pl.pallas_call(kernel, out_shape=(jax.ShapeDtypeStruct((CR, TR, TC), BF16...  37.1 us
    pallas_call x1, Pallas kernels, body(): pl.pallas_call(finish, out_shape=(pltpu.HBM((1, CR, TR, TC), BF16), pltpu...  1.08 us

profile of v2, /device:TPU:1, one launch (start us, length us, event | category | flops | bytes accessed | tf_op | source)
XLA Modules:
  0.0 39.5 jit_solution(5806394468882649645)
XLA Ops:
  1.3 37.1 %shard_map.102 = (bf16[99,16,128]{2,1,0:T(8,128)(2,1)S(1)}, bf16[2,16,64,128]{3,2,1,0:T(8,128)(2,1)S(1)}, f32[2,80,128]{2,1,0:T(8,128)S(1)}) custom-call(bf16[1,172,16,128]{3,2,1,0:T(8,128)(2,1)} %saved_hbm.1, bf16[1,128,16,128]{3,2,1,0:T(8,128)(2,1)} %pre_hbm.1, bf16[1,128,16,128]{3,2,1,0:T(8,128)(2,1)} %cot_hbm.1, bf16[9,172,128]{2,1,0:T(8,128)(2,1)} %w_hbm.1, ...), custom_call_target="tpu_custom_call" | custom-call | flops 1623195648 | bytes 4194304 | tf_op jit(solution)/shard_map/pallas_call | solution.py:426
  38.4 1.1 %shard_map.103 = (bf16[1,99,16,128]{3,2,1,0:T(8,128)(2,1)}, f32[9,172,128]{2,1,0:T(8,128)}, f32[128]{0:T(128)}, f32[73,2,128]{2,1,0:T(2,128)}) custom-call(bf16[99,16,128]{2,1,0:T(8,128)(2,1)S(1)} %get-tuple-element.11.ig_v, bf16[2,16,64,128]{3,2,1,0:T(8,128)(2,1)S(1)} %get-tuple-element.12.gbuf, f32[2,80,128]{2,1,0:T(8,128)S(1)} %get-tuple-element.13.gg_v), custom_call_target="tpu_custom_call" | custom-call | tf_op jit(solution)/shard_map/pallas_call | solution.py:489

commit v3 on v2

--- a/solution.py
+++ b/solution.py
@@ -25,6 +25,7 @@
 PITCH = TOP + TC + 8
 BLK = 80
 SCALE_NORM = 1.0 / math.sqrt(512 * 512 * 2)
+PLANE = (10, 9, 11, 6, 14, 8, 2, 5, 7, 13, 15, 4, 12, 1, 3)
 MESH = pl.DeviceIdType.MESH
 F32 = jnp.float32
 BF16 = jnp.bfloat16
@@ -35,7 +36,7 @@
     ig_v, gbuf, ggrad_ref,
     saved_v, pre_v, cot_v, w_v, interp_v, targets_ref,
     d32, s32, p32, dzc, smat, wcat, colbuf, colrecv, corner,
-    pick, edge, lpad, extra,
+    rows_out, rows_in, pick, edge, lpad, extra,
     awh, crecv, acc, xrecv, zbuf,
     bk32, cmask, glob_out, glob_recv, own, cplrecv,
     in_sem, halo_ss, halo_rs, core_ss, core_rs, xy_ss, xy_rs, z_ss, z_rs,
@@ -141,35 +142,6 @@
         total = total + turn(i)
     bias = jnp.sum(total, axis=0, keepdims=True)
 
-    pl.semaphore_wait(barrier, 8 + 3 + 1 + 1 + 15 + 7)
-
-    for dr, dg in halo_steps:
-        row = TR if dr > 0 else 1
-        if dg == 0:
-            kind = 0
-            src = p32.at[row, pl.ds(TOP, TC)]
-            dst = p32.at[0 if dr > 0 else TR + 1, pl.ds(TOP, TC)]
-        elif dr == 0:
-            kind = 1
-            src = colbuf.at[1 if dg > 0 else 0]
-            dst = colrecv.at[0 if dg > 0 else 1]
-        else:
-            kind = 2
-            src = p32.at[row, pl.ds(TOP + TC - 8 if dg > 0 else TOP, 8)]
-            dst = corner.at[0 if dr > 0 else 1, 0 if dg > 0 else 1]
-        pltpu.make_async_remote_copy(
-            src, dst, halo_ss.at[kind], halo_rs.at[kind],
-            device_id=halo_dev(dr, dg), device_id_type=MESH,
-        ).start()
-
-    def bulk(ref, sem):
-        return pltpu.make_async_copy(ref, ref, sem).wait
-
-    halo_bulk = (d32.at[pl.ds(0, 2 * TC)], colrecv, corner)
-    for kind in range(3):
-        pend["halo_s", kind] = bulk(halo_bulk[kind], halo_ss.at[kind])
-        pend["halo", kind] = bulk(halo_bulk[kind], halo_rs.at[kind])
-
     pend.pop(2)()
 
     def saved_step(n, carry):
@@ -178,6 +150,29 @@
         return carry
 
     lax.fori_loop(0, CIN // 4, saved_step, 0)
+    rows_out[0] = s32[pl.ds(0, CPAD, stride=TR), :].astype(BF16)
+    rows_out[1] = s32[pl.ds(TR - 1, CPAD, stride=TR), :].astype(BF16)
+
+    pl.semaphore_wait(barrier, 8 + 3 + 1 + 1 + 15 + 7)
+
+    def send(src, dst, kind, dr, dg):
+        pltpu.make_async_remote_copy(
+            src, dst, halo_ss.at[kind], halo_rs.at[kind],
+            device_id=halo_dev(dr, dg), device_id_type=MESH,
+        ).start()
+
+    def bulk(ref, sem):
+        return pltpu.make_async_copy(ref, ref, sem).wait
+
+    send(rows_out.at[0], rows_in.at[1], 0, -1, 0)
+    send(rows_out.at[1], rows_in.at[0], 0, 1, 0)
+    send(colbuf.at[0], colrecv.at[1], 1, 0, -1)
+    send(colbuf.at[1], colrecv.at[0], 1, 0, 1)
+    halo_bulk = (rows_in, colrecv, d32.at[pl.ds(0, 2 * TC)], corner)
+    for kind in range(4):
+        pend["halo_s", kind] = bulk(halo_bulk[kind], halo_ss.at[kind])
+        pend["halo", kind] = bulk(halo_bulk[kind], halo_rs.at[kind])
+
     for i in range(TR):
         smat[:, i * TC : (i + 1) * TC] = s32[pl.ds(i, CPAD, stride=TR), :].astype(BF16)
 
@@ -188,12 +183,11 @@
             ].astype(BF16)
 
     lax.fori_loop(1, TR + 1, lambda i, c: (shift_rows(i), c)[1], 0)
-    border = jnp.zeros((TC, 3 * CH), BF16)
-    dzc[:TC, :] = border
-    dzc[(TR + 1) * TC :, :] = border
     for a in range(3):
+        first, count = max(a - 1, 0), TR - abs(a - 1)
+        start = TC * (first + 2 - a)
         term = jnp.dot(
-            smat[...], dzc[(2 - a) * TC : (2 - a) * TC + TR * TC, :],
+            smat[:, first * TC : (first + count) * TC], dzc[start : start + count * TC, :],
             preferred_element_type=F32,
         )
         for bi in range(3):
@@ -202,7 +196,15 @@
                 awh[h, k * HALF : (k + 1) * HALF, :] = term[
                     h * HALF : (h + 1) * HALF, bi * CH : (bi + 1) * CH
                 ]
-    awh[1, CIN - HALF : CIN - HALF + 1, :] = bias
+
+    for dr, dg in halo_steps:
+        row = TR if dr > 0 else 1
+        if dg == 0:
+            dst = p32.at[0 if dr > 0 else TR + 1, pl.ds(TOP, TC)]
+            send(p32.at[row, pl.ds(TOP, TC)], dst, 2, dr, dg)
+        elif dr != 0:
+            dst = corner.at[0 if dr > 0 else 1, 0 if dg > 0 else 1]
+            send(p32.at[row, pl.ds(TOP + TC - 8 if dg > 0 else TOP, 8)], dst, 3, dr, dg)
 
     at_row = lax.broadcasted_iota(jnp.int32, (TC, TC), 0)
     at_lane = lax.broadcasted_iota(jnp.int32, (TC, TC), 1)
@@ -212,30 +214,19 @@
         pick[i * TC : (i + 1) * TC, :] = jnp.where(first | last, 1.0, 0.0).astype(BF16)
     edge[...] = jnp.dot(smat[...], pick[...], preferred_element_type=F32).astype(BF16)
 
-    pend.pop(3)()
-    for a in range(3):
-        for bi in range(3):
-            wcat[a, :CIN, bi * CH : (bi + 1) * CH] = w_v[3 * a + bi]
-
-    for kind in range(3):
-        pend.pop(("halo", kind))()
+    pend.pop(("halo", 0))()
+    pend.pop(("halo", 1))()
     up = (reg > 0).astype(F32)
     down = (reg < 31).astype(F32)
     left = (glob > 0).astype(F32)
     right = (glob < 3).astype(F32)
-    p32[0, TOP : TOP + TC, :] = p32[0, TOP : TOP + TC, :] * up
-    p32[TR + 1, TOP : TOP + TC, :] = p32[TR + 1, TOP : TOP + TC, :] * down
     lpad[0, 1 : TR + 1, :] = colrecv[0] * left
     lpad[1, 1 : TR + 1, :] = colrecv[1] * right
     for i in range(TR):
         p32[i + 1, TOP - 1 : TOP, :] = lpad[0, i + 1 : i + 2, :]
         p32[i + 1, TOP + TC : TOP + TC + 1, :] = lpad[1, i + 1 : i + 2, :]
-    p32[0, TOP - 1 : TOP, :] = corner[0, 0, 7:8, :] * (up * left)
-    p32[0, TOP + TC : TOP + TC + 1, :] = corner[0, 1, 0:1, :] * (up * right)
-    p32[TR + 1, TOP - 1 : TOP, :] = corner[1, 0, 7:8, :] * (down * left)
-    p32[TR + 1, TOP + TC : TOP + TC + 1, :] = corner[1, 1, 0:1, :] * (down * right)
-    shift_rows(0)
-    shift_rows(TR + 1)
+    shift_rows(1)
+    shift_rows(TR)
     for a in range(3):
         extra[a, :TR, 2 * CH :] = lpad[0, 2 - a : 2 - a + TR, :].astype(BF16)
         extra[a, TR : 2 * TR, :CH] = lpad[1, 2 - a : 2 - a + TR, :].astype(BF16)
@@ -243,11 +234,13 @@
     for a in range(3):
         term = jnp.dot(edge[...], extra[a], preferred_element_type=F32)
         if a == 0:
-            term = term + jnp.dot(
-                smat[:, (TR - 1) * TC :], dzc[(TR + 1) * TC :, :], preferred_element_type=F32
+            term = term + up * jnp.dot(
+                rows_in[0], dzc[TC : 2 * TC, :], preferred_element_type=F32
             )
         if a == 2:
-            term = term + jnp.dot(smat[:, :TC], dzc[:TC, :], preferred_element_type=F32)
+            term = term + down * jnp.dot(
+                rows_in[1], dzc[TR * TC : (TR + 1) * TC, :], preferred_element_type=F32
+            )
         for bi in range(3):
             k = 3 * a + bi
             for h in range(2):
@@ -264,22 +257,22 @@
         ).start()
     pend["core_s"] = bulk(crecv.at[pl.ds(0, ROWS_HALF)], core_ss)
     pend["core"] = bulk(crecv.at[pl.ds(0, ROWS_HALF)], core_rs)
-    lax.fori_loop(1, TR + 1, lambda i, c: (shift_rows(i), c)[1], 0)
     pend.pop("core")()
     acc[:ROWS_PAD, :] = (awh[core] + crecv[...]).astype(BF16)
-    def xy_start(n, carry):
-        d = 15 - n
+    for d in PLANE:
         px, py = plane(d)
         pltpu.make_async_remote_copy(
             acc.at[pl.ds(pl.multiple_of((px * 4 + py) * PIECE, PIECE), PIECE)],
             xrecv.at[d], xy_ss, xy_rs,
             device_id=at(px, py, z, core), device_id_type=MESH,
         ).start()
-        return carry
-
-    lax.fori_loop(0, 15, xy_start, 0)
     pend["xy_s"] = bulk(xrecv.at[pl.ds(1, 15)], xy_ss)
     pend["xy"] = bulk(xrecv.at[pl.ds(1, 15)], xy_rs)
+    pend.pop(3)()
+    for a in range(3):
+        for bi in range(3):
+            wcat[a, :CIN, bi * CH : (bi + 1) * CH] = w_v[3 * a + bi]
+    lax.fori_loop(2, TR, lambda i, c: (shift_rows(i), c)[1], 0)
 
     level = jnp.full((1, TC), noise_ref[0], jnp.int32).astype(F32) / (NOISE_LEVELS - 1)
     sigma = jnp.exp(math.log(2.0) + level * (math.log(0.05) - math.log(2.0)))
@@ -299,7 +292,34 @@
             d32[pl.ds(2 * n + half, CR, stride=TR), :] = part[:CR] * scale
         return carry
 
-    lax.fori_loop(0, TR // 2, back_step, 0)
+    lax.fori_loop(1, TR // 2 - 1, back_step, 0)
+
+    pend.pop("xy")()
+    piece = acc[pl.ds(pl.multiple_of(q * PIECE, PIECE), PIECE), :].astype(F32)
+    for d in range(1, 16):
+        piece = piece + xrecv[d].astype(F32)
+    zbuf[z] = piece.astype(BF16)
+
+    for d in (4, 3, 5, 2, 6, 1, 7):
+        pltpu.make_async_remote_copy(
+            zbuf.at[z], zbuf.at[z], z_ss, z_rs, device_id=z_dev(d), device_id_type=MESH
+        ).start()
+    pend["z_s"] = bulk(zbuf.at[pl.ds(0, 7)], z_ss)
+    pend["z"] = bulk(zbuf.at[pl.ds(0, 7)], z_rs)
+
+    pend.pop(("halo", 2))()
+    pend.pop(("halo", 3))()
+    p32[0, TOP : TOP + TC, :] = p32[0, TOP : TOP + TC, :] * up
+    p32[TR + 1, TOP : TOP + TC, :] = p32[TR + 1, TOP : TOP + TC, :] * down
+    p32[0, TOP - 1 : TOP, :] = corner[0, 0, 7:8, :] * (up * left)
+    p32[0, TOP + TC : TOP + TC + 1, :] = corner[0, 1, 0:1, :] * (up * right)
+    p32[TR + 1, TOP - 1 : TOP, :] = corner[1, 0, 7:8, :] * (down * left)
+    p32[TR + 1, TOP + TC : TOP + TC + 1, :] = corner[1, 1, 0:1, :] * (down * right)
+    shift_rows(0)
+    shift_rows(TR + 1)
+
+    back_step(0, 0)
+    back_step(TR // 2 - 1, 0)
 
     def igrad_step(n, carry):
         rows = d32[pl.ds(pl.multiple_of(n * 9 * TR, 16), 9 * TR), :]
@@ -327,21 +347,18 @@
         ).start()
     pend["glob_s"] = bulk(glob_recv, gl_ss.at[0])
     pend["glob"] = bulk(glob_recv, gl_rs.at[0])
-    pend.pop("xy")()
-    piece = acc[pl.ds(pl.multiple_of(q * PIECE, PIECE), PIECE), :].astype(F32)
-    for d in range(1, 16):
-        piece = piece + xrecv[d].astype(F32)
-    zbuf[z] = piece.astype(BF16)
-
-    def z_start(d, carry):
-        pltpu.make_async_remote_copy(
-            zbuf.at[z], zbuf.at[z], z_ss, z_rs, device_id=z_dev(d), device_id_type=MESH
-        ).start()
-        return carry
-
-    lax.fori_loop(1, 8, z_start, 0)
-    pend["z_s"] = bulk(zbuf.at[pl.ds(0, 7)], z_ss)
-    pend["z"] = bulk(zbuf.at[pl.ds(0, 7)], z_rs)
+    pend.pop("z")()
+    full = zbuf[0].astype(F32)
+    for n in range(1, 8):
+        full = full + zbuf[n].astype(F32)
+    gbuf[core, q] = (full * SCALE_NORM).astype(BF16)
+
+    for d in PLANE:
+        pltpu.make_async_remote_copy(
+            gbuf.at[core, q], gbuf.at[core, q], ag_ss, ag_rs.at[d // 4],
+            device_id=plane_dev(d), device_id_type=MESH,
+        ).start()
+    pend["ag_s"] = bulk(gbuf.at[0, pl.ds(0, 15)], ag_ss)
 
     pend.pop("glob")()
     own[0] = glob_out[1] + glob_recv[1] + glob_recv[2]
@@ -353,26 +370,6 @@
     pend["cpl_s"] = cpl_copy.wait_send
     pend["cpl"] = cpl_copy.wait_recv
 
-    pend.pop("z")()
-    full = zbuf[0].astype(F32)
-    for n in range(1, 8):
-        full = full + zbuf[n].astype(F32)
-    gbuf[core, q] = (full * SCALE_NORM).astype(BF16)
-
-    def ag_start(n, carry):
-        d = 15 - n
-        pltpu.make_async_remote_copy(
-            gbuf.at[core, q], gbuf.at[core, q], ag_ss, ag_rs.at[d // 4],
-            device_id=plane_dev(d), device_id_type=MESH,
-        ).start()
-        return carry
-
-    lax.fori_loop(0, 15, ag_start, 0)
-    pend["ag_s"] = bulk(gbuf.at[0, pl.ds(0, 15)], ag_ss)
-
-    pend.pop("cpl")()
-    ggrad_ref[...] = own[...] + cplrecv[...]
-
     for dx in (0, 1, 3, 2):
         count = 3 if dx == 0 else 4
         bulk(gbuf.at[0, pl.ds(0, count)], ag_rs.at[dx])()
@@ -381,6 +378,8 @@
             column, column, fw_ss, fw_rs, device_id=sibling, device_id_type=MESH
         ).start()
     pend["fw_s"] = bulk(gbuf.at[0], fw_ss)
+    pend.pop("cpl")()
+    ggrad_ref[...] = own[...] + cplrecv[...]
     bulk(gbuf.at[0], fw_rs)()
     for wait in pend.values():
         wait()
@@ -448,6 +447,8 @@
             pltpu.VMEM((2, TR, CH), F32),
             pltpu.VMEM((2, TR, CH), F32),
             pltpu.VMEM((2, 2, 8, CH), F32),
+            pltpu.VMEM((2, CPAD, TC), BF16),
+            pltpu.VMEM((2, CPAD, TC), BF16),
             pltpu.VMEM((TR * TC, TC), BF16),
             pltpu.VMEM((CPAD, TC), BF16),
             pltpu.VMEM((2, 24, CH), F32),
@@ -464,8 +465,8 @@
             pltpu.VMEM((2, BLK, TC), F32),
             pltpu.VMEM((2, BLK, TC), F32),
             dma((6,)),
-            dma((3,)),
-            dma((3,)),
+            dma((4,)),
+            dma((4,)),
             dma,
             dma,
             dma,

time: 39.6 us -> 38.3 us (0.967)
  Pallas kernels: 38.2 us -> 36.9 us
    pallas_call x1, Pallas kernels: 37.1 us -> 35.8 us  [body(): pl.pallas_call(kernel, out_shape=(jax.ShapeDtypeStruct((CR, TR, TC), BF16...]
where the time goes in v3:
time: 38.3 us; the launch traced here: 38.2 us
  Pallas kernels  36.9 us (96%)
  between operations  1.29 us (3%)
    pallas_call x1, Pallas kernels, body(): pl.pallas_call(kernel, out_shape=(jax.ShapeDtypeStruct((CR, TR, TC), BF16...  35.8 us
    pallas_call x1, Pallas kernels, body(): pl.pallas_call(finish, out_shape=(pltpu.HBM((1, CR, TR, TC), BF16), pltpu...  1.08 us

profile of v3, /device:TPU:1, one launch (start us, length us, event | category | flops | bytes accessed | tf_op | source)
XLA Modules:
  0.0 38.2 jit_solution(17215116710882468392)
XLA Ops:
  1.3 35.8 %shard_map.102 = (bf16[99,16,128]{2,1,0:T(8,128)(2,1)S(1)}, bf16[2,16,64,128]{3,2,1,0:T(8,128)(2,1)S(1)}, f32[2,80,128]{2,1,0:T(8,128)S(1)}) custom-call(bf16[1,172,16,128]{3,2,1,0:T(8,128)(2,1)} %saved_hbm.1, bf16[1,128,16,128]{3,2,1,0:T(8,128)(2,1)} %pre_hbm.1, bf16[1,128,16,128]{3,2,1,0:T(8,128)(2,1)} %cot_hbm.1, bf16[9,172,128]{2,1,0:T(8,128)(2,1)} %w_hbm.1, ...), custom_call_target="tpu_custom_call" | custom-call | flops 1623195648 | bytes 4194304 | tf_op jit(solution)/shard_map/pallas_call | solution.py:425
  37.1 1.1 %shard_map.103 = (bf16[1,99,16,128]{3,2,1,0:T(8,128)(2,1)}, f32[9,172,128]{2,1,0:T(8,128)}, f32[128]{0:T(128)}, f32[73,2,128]{2,1,0:T(2,128)}) custom-call(bf16[99,16,128]{2,1,0:T(8,128)(2,1)S(1)} %get-tuple-element.11.ig_v, bf16[2,16,64,128]{3,2,1,0:T(8,128)(2,1)S(1)} %get-tuple-element.12.gbuf, f32[2,80,128]{2,1,0:T(8,128)S(1)} %get-tuple-element.13.gg_v), custom_call_target="tpu_custom_call" | custom-call | tf_op jit(solution)/shard_map/pallas_call | solution.py:490

commit v4 on v3

--- a/solution.py
+++ b/solution.py
@@ -26,6 +26,7 @@
 BLK = 80
 SCALE_NORM = 1.0 / math.sqrt(512 * 512 * 2)
 PLANE = (10, 9, 11, 6, 14, 8, 2, 5, 7, 13, 15, 4, 12, 1, 3)
+ZLINE = (4, 3, 5, 2, 6, 1, 7)
 MESH = pl.DeviceIdType.MESH
 F32 = jnp.float32
 BF16 = jnp.bfloat16
@@ -86,24 +87,27 @@
             (targets_hbm, targets_ref),
         ))
     ]
+    barrier = pltpu.get_barrier_semaphore()
+
+    def greet(device):
+        pl.semaphore_signal(barrier, inc=1, device_id=device, device_id_type=MESH)
+
+    halo_steps = [(dr, dg) for dr in (-1, 0, 1) for dg in (-1, 0, 1) if dr or dg]
+    greet(flat_dev(64))
+    for d in ZLINE:
+        greet(z_dev(d))
     for load in loads:
         load.start()
     pend = {n: load.wait for n, load in enumerate(loads)}
 
-    barrier = pltpu.get_barrier_semaphore()
-
-    def greet(device):
-        pl.semaphore_signal(barrier, inc=1, device_id=device, device_id_type=MESH)
-
-    halo_steps = [(dr, dg) for dr in (-1, 0, 1) for dg in (-1, 0, 1) if dr or dg]
+    for d in PLANE:
+        greet(plane_dev(d))
     for dr, dg in halo_steps:
         greet(halo_dev(dr, dg))
-    for step in (-1, 1, 64):
+    for step in (-1, 1):
         greet(flat_dev(step))
     greet(other)
     greet(sibling)
-    lax.fori_loop(1, 16, lambda d, c: (greet(plane_dev(d)), c)[1], 0)
-    lax.fori_loop(1, 8, lambda d, c: (greet(z_dev(d)), c)[1], 0)
 
     s32[CIN * TR :, :] = jnp.zeros((CPAD * TR - CIN * TR, TC), F32)
     wcat[:, CPAD - 16 :, :] = jnp.zeros((3, 16, 3 * CH), BF16)
@@ -300,7 +304,7 @@
         piece = piece + xrecv[d].astype(F32)
     zbuf[z] = piece.astype(BF16)
 
-    for d in (4, 3, 5, 2, 6, 1, 7):
+    for d in ZLINE:
         pltpu.make_async_remote_copy(
             zbuf.at[z], zbuf.at[z], z_ss, z_rs, device_id=z_dev(d), device_id_type=MESH
         ).start()

time: 38.3 us -> 36.8 us (0.961)
  Pallas kernels: 36.9 us -> 35.4 us
    pallas_call x1, Pallas kernels: 35.8 us -> 34.3 us  [body(): pl.pallas_call(kernel, out_shape=(jax.ShapeDtypeStruct((CR, TR, TC), BF16...]
where the time goes in v4:
time: 36.8 us; the launch traced here: 36.6 us
  Pallas kernels  35.4 us (96%)
  between operations  1.29 us (4%)
    pallas_call x1, Pallas kernels, body(): pl.pallas_call(kernel, out_shape=(jax.ShapeDtypeStruct((CR, TR, TC), BF16...  34.3 us
    pallas_call x1, Pallas kernels, body(): pl.pallas_call(finish, out_shape=(pltpu.HBM((1, CR, TR, TC), BF16), pltpu...  1.08 us

profile of v4, /device:TPU:1, one launch (start us, length us, event | category | flops | bytes accessed | tf_op | source)
XLA Modules:
  0.0 36.6 jit_solution(11858450000432482049)
XLA Ops:
  1.3 34.3 %shard_map.102 = (bf16[99,16,128]{2,1,0:T(8,128)(2,1)S(1)}, bf16[2,16,64,128]{3,2,1,0:T(8,128)(2,1)S(1)}, f32[2,80,128]{2,1,0:T(8,128)S(1)}) custom-call(bf16[1,172,16,128]{3,2,1,0:T(8,128)(2,1)} %saved_hbm.1, bf16[1,128,16,128]{3,2,1,0:T(8,128)(2,1)} %pre_hbm.1, bf16[1,128,16,128]{3,2,1,0:T(8,128)(2,1)} %cot_hbm.1, bf16[9,172,128]{2,1,0:T(8,128)(2,1)} %w_hbm.1, ...), custom_call_target="tpu_custom_call" | custom-call | flops 1623195648 | bytes 4194304 | tf_op jit(solution)/shard_map/pallas_call | solution.py:429
  35.6 1.1 %shard_map.103 = (bf16[1,99,16,128]{3,2,1,0:T(8,128)(2,1)}, f32[9,172,128]{2,1,0:T(8,128)}, f32[128]{0:T(128)}, f32[73,2,128]{2,1,0:T(2,128)}) custom-call(bf16[99,16,128]{2,1,0:T(8,128)(2,1)S(1)} %get-tuple-element.11.ig_v, bf16[2,16,64,128]{3,2,1,0:T(8,128)(2,1)S(1)} %get-tuple-element.12.gbuf, f32[2,80,128]{2,1,0:T(8,128)S(1)} %get-tuple-element.13.gg_v), custom_call_target="tpu_custom_call" | custom-call | tf_op jit(solution)/shard_map/pallas_call | solution.py:494

commit v5 on v4

--- a/solution.py
+++ b/solution.py
@@ -37,7 +37,7 @@
     ig_v, gbuf, ggrad_ref,
     saved_v, pre_v, cot_v, w_v, interp_v, targets_ref,
     d32, s32, p32, dzc, smat, wcat, colbuf, colrecv, corner,
-    rows_out, rows_in, pick, edge, lpad, extra,
+    rows_out, sides, pick, lpad, extra,
     awh, crecv, acc, xrecv, zbuf,
     bk32, cmask, glob_out, glob_recv, own, cplrecv,
     in_sem, halo_ss, halo_rs, core_ss, core_rs, xy_ss, xy_rs, z_ss, z_rs,
@@ -118,7 +118,7 @@
         p32[i + 1, :TOP, :] = jnp.zeros((TOP, CH), F32)
         p32[i + 1, TOP + TC :, :] = jnp.zeros((8, CH), F32)
     lpad[...] = jnp.zeros((2, 24, CH), F32)
-    extra[...] = jnp.zeros((3, TC, 3 * CH), BF16)
+    extra[:, :TC, :] = jnp.zeros((3, TC, 3 * CH), BF16)
     bk32[:, CPAD:, :] = jnp.zeros((TR, 8, TC), F32)
 
     pend.pop(0)()
@@ -168,11 +168,11 @@
     def bulk(ref, sem):
         return pltpu.make_async_copy(ref, ref, sem).wait
 
-    send(rows_out.at[0], rows_in.at[1], 0, -1, 0)
-    send(rows_out.at[1], rows_in.at[0], 0, 1, 0)
+    send(rows_out.at[0], sides.at[2, :, pl.ds(TC, TC)], 0, -1, 0)
+    send(rows_out.at[1], sides.at[0, :, pl.ds(TC, TC)], 0, 1, 0)
     send(colbuf.at[0], colrecv.at[1], 1, 0, -1)
     send(colbuf.at[1], colrecv.at[0], 1, 0, 1)
-    halo_bulk = (rows_in, colrecv, d32.at[pl.ds(0, 2 * TC)], corner)
+    halo_bulk = (rows_out, colrecv, d32.at[pl.ds(0, 2 * TC)], corner)
     for kind in range(4):
         pend["halo_s", kind] = bulk(halo_bulk[kind], halo_ss.at[kind])
         pend["halo", kind] = bulk(halo_bulk[kind], halo_rs.at[kind])
@@ -216,7 +216,14 @@
         first = (at_row == 0) & (at_lane == i)
         last = (at_row == TC - 1) & (at_lane == TR + i)
         pick[i * TC : (i + 1) * TC, :] = jnp.where(first | last, 1.0, 0.0).astype(BF16)
-    edge[...] = jnp.dot(smat[...], pick[...], preferred_element_type=F32).astype(BF16)
+    edge = jnp.dot(smat[...], pick[...], preferred_element_type=F32).astype(BF16)
+    for a in range(3):
+        sides[a, :, :TC] = edge
+
+    pend.pop(3)()
+    for a in range(3):
+        for bi in range(3):
+            wcat[a, :CIN, bi * CH : (bi + 1) * CH] = w_v[3 * a + bi]
 
     pend.pop(("halo", 0))()
     pend.pop(("halo", 1))()
@@ -229,22 +236,20 @@
     for i in range(TR):
         p32[i + 1, TOP - 1 : TOP, :] = lpad[0, i + 1 : i + 2, :]
         p32[i + 1, TOP + TC : TOP + TC + 1, :] = lpad[1, i + 1 : i + 2, :]
-    shift_rows(1)
-    shift_rows(TR)
+    for a, row, there in ((0, 1, up), (2, TR, down)):
+        for bi in range(3):
+            extra[a, TC:, bi * CH : (bi + 1) * CH] = (
+                there * p32[row, TOP + 1 - bi : TOP + 1 - bi + TC, :]
+            ).astype(BF16)
     for a in range(3):
         extra[a, :TR, 2 * CH :] = lpad[0, 2 - a : 2 - a + TR, :].astype(BF16)
         extra[a, TR : 2 * TR, :CH] = lpad[1, 2 - a : 2 - a + TR, :].astype(BF16)
 
-    for a in range(3):
-        term = jnp.dot(edge[...], extra[a], preferred_element_type=F32)
-        if a == 0:
-            term = term + up * jnp.dot(
-                rows_in[0], dzc[TC : 2 * TC, :], preferred_element_type=F32
-            )
-        if a == 2:
-            term = term + down * jnp.dot(
-                rows_in[1], dzc[TR * TC : (TR + 1) * TC, :], preferred_element_type=F32
-            )
+    for a in (1, 0, 2):
+        depth = TC if a == 1 else 2 * TC
+        term = jnp.dot(
+            sides[a, :, :depth], extra[a, :depth, :], preferred_element_type=F32
+        )
         for bi in range(3):
             k = 3 * a + bi
             for h in range(2):
@@ -272,11 +277,7 @@
         ).start()
     pend["xy_s"] = bulk(xrecv.at[pl.ds(1, 15)], xy_ss)
     pend["xy"] = bulk(xrecv.at[pl.ds(1, 15)], xy_rs)
-    pend.pop(3)()
-    for a in range(3):
-        for bi in range(3):
-            wcat[a, :CIN, bi * CH : (bi + 1) * CH] = w_v[3 * a + bi]
-    lax.fori_loop(2, TR, lambda i, c: (shift_rows(i), c)[1], 0)
+    lax.fori_loop(1, TR + 1, lambda i, c: (shift_rows(i), c)[1], 0)
 
     level = jnp.full((1, TC), noise_ref[0], jnp.int32).astype(F32) / (NOISE_LEVELS - 1)
     sigma = jnp.exp(math.log(2.0) + level * (math.log(0.05) - math.log(2.0)))
@@ -325,12 +326,6 @@
     back_step(0, 0)
     back_step(TR // 2 - 1, 0)
 
-    def igrad_step(n, carry):
-        rows = d32[pl.ds(pl.multiple_of(n * 9 * TR, 16), 9 * TR), :]
-        ig_v[pl.ds(n * 9, 9)] = rows.reshape(9, TR, TC).astype(BF16)
-        return carry
-
-    lax.fori_loop(0, CR // 9, igrad_step, 0)
     pend.pop(5)()
     home = (reg * 4 + glob) * 2
     wanted = [(home + step + NGB) % NGB for step in (-1, 0, 1, 2, NGB // 2)]
@@ -364,6 +359,12 @@
         ).start()
     pend["ag_s"] = bulk(gbuf.at[0, pl.ds(0, 15)], ag_ss)
 
+    def igrad_step(n, carry):
+        rows = d32[pl.ds(pl.multiple_of(n * 9 * TR, 16), 9 * TR), :]
+        ig_v[pl.ds(n * 9, 9)] = rows.reshape(9, TR, TC).astype(BF16)
+        return carry
+
+    lax.fori_loop(0, CR // 9, igrad_step, 0)
     pend.pop("glob")()
     own[0] = glob_out[1] + glob_recv[1] + glob_recv[2]
     own[1] = glob_out[2] + glob_recv[0]
@@ -452,11 +453,10 @@
             pltpu.VMEM((2, TR, CH), F32),
             pltpu.VMEM((2, 2, 8, CH), F32),
             pltpu.VMEM((2, CPAD, TC), BF16),
-            pltpu.VMEM((2, CPAD, TC), BF16),
+            pltpu.VMEM((3, CPAD, 2 * TC), BF16),
             pltpu.VMEM((TR * TC, TC), BF16),
-            pltpu.VMEM((CPAD, TC), BF16),
             pltpu.VMEM((2, 24, CH), F32),
-            pltpu.VMEM((3, TC, 3 * CH), BF16),
+            pltpu.VMEM((3, 2 * TC, 3 * CH), BF16),
             pltpu.VMEM((2, ROWS_PAD, CH), F32),
             pltpu.VMEM((ROWS_PAD, CH), F32),
             pltpu.VMEM((ROWS_ALL, CH), BF16),

time: 36.8 us -> 36.6 us (level)
  no operation moved by 1% of the time
where the time goes in v5:
time: 36.6 us; the launch traced here: 36.5 us
  Pallas kernels  35.2 us (96%)
  between operations  1.29 us (4%)
    pallas_call x1, Pallas kernels, body(): pl.pallas_call(kernel, out_shape=(jax.ShapeDtypeStruct((CR, TR, TC), BF16...  34.2 us
    pallas_call x1, Pallas kernels, body(): pl.pallas_call(finish, out_shape=(pltpu.HBM((1, CR, TR, TC), BF16), pltpu...  1.08 us

profile of v5, /device:TPU:1, one launch (start us, length us, event | category | flops | bytes accessed | tf_op | source)
XLA Modules:
  0.0 36.5 jit_solution(2954747165213651936)
XLA Ops:
  1.3 34.2 %shard_map.102 = (bf16[99,16,128]{2,1,0:T(8,128)(2,1)S(1)}, bf16[2,16,64,128]{3,2,1,0:T(8,128)(2,1)S(1)}, f32[2,80,128]{2,1,0:T(8,128)S(1)}) custom-call(bf16[1,172,16,128]{3,2,1,0:T(8,128)(2,1)} %saved_hbm.1, bf16[1,128,16,128]{3,2,1,0:T(8,128)(2,1)} %pre_hbm.1, bf16[1,128,16,128]{3,2,1,0:T(8,128)(2,1)} %cot_hbm.1, bf16[9,172,128]{2,1,0:T(8,128)(2,1)} %w_hbm.1, ...), custom_call_target="tpu_custom_call" | custom-call | flops 1623195648 | bytes 4194304 | tf_op jit(solution)/shard_map/pallas_call | solution.py:430
  35.5 1.1 %shard_map.103 = (bf16[1,99,16,128]{3,2,1,0:T(8,128)(2,1)}, f32[9,172,128]{2,1,0:T(8,128)}, f32[128]{0:T(128)}, f32[73,2,128]{2,1,0:T(2,128)}) custom-call(bf16[99,16,128]{2,1,0:T(8,128)(2,1)S(1)} %get-tuple-element.11.ig_v, bf16[2,16,64,128]{3,2,1,0:T(8,128)(2,1)S(1)} %get-tuple-element.12.gbuf, f32[2,80,128]{2,1,0:T(8,128)S(1)} %get-tuple-element.13.gg_v), custom_call_target="tpu_custom_call" | custom-call | tf_op jit(solution)/shard_map/pallas_call | solution.py:494
